TPU v7x, 128 devices: a whole 4x4x4 slice. The times are simulated.
128 devices in a mesh: row: 8 (over y, core), col: 16 (over z, x).
Axes of the slice: x: 4, y: 4, z: 4, core: 2. Of those that a mesh axis runs over, the one named last changes fastest.
Arguments:
- latents: bfloat16 [32768, 1024], P(('row', 'col')), may hold values from -24 to 24
- noise: bfloat16 [32768, 1024], P(('col', 'row')), may hold values from -6 to 6
- pairing: int32 [32768], P('row'), may hold values from 0 to 32767, as said below
- time_bucket: int32 [32768], P(('row', 'col')), may hold values from 0 to 999
Outputs:
- potential_f: float32 [32768], P(('row', 'col'))
- potential_g: float32 [32768], P(('col', 'row'))
- interpolant: bfloat16 [32768, 1024], P(('row', 'col'))
- log_weight: float32 [32768], P(('row', 'col'))
Inputs may be any that keep to these rules, and one draw needn't show every extreme that they name: pairing is a permutation of 0..32767. Cut the latents into aligned blocks of 256 and the noise draws into aligned blocks of 2048: at most 32 latents of one latent block are paired with one noise block, and this many are reached.
All inputs are finite; a program needn't handle non-finite values.
Results may differ from a plain program's by a relative error of at most 0.001.
Values may be sent and summed in bfloat16 or wider, within the bound.
A program may use at most 128 MiB of HBM per device.

v0:
```python
import math

import jax
import jax.numpy as jnp
from jax import lax
from jax.sharding import PartitionSpec as P

ITERS = 4
BUCKETS = 1000


entropic = 0.1


def row_update(cost, potential, offset):
    scores = (potential[None, :] - cost) / entropic
    peak = lax.pmax(jnp.max(scores, axis=1), "col")
    running = lax.psum(jnp.sum(jnp.exp(scores - peak[:, None]), axis=1), "col")
    return -entropic * (peak + jnp.log(running)) - offset


def column_update(cost, potential, offset):
    scores = (potential[:, None] - cost) / entropic
    peak = lax.pmax(jnp.max(scores, axis=0), "row")
    running = lax.psum(jnp.sum(jnp.exp(scores - peak[None, :]), axis=0), "row")
    return -entropic * (peak + jnp.log(running)) - offset


def shards(latents, noise, pairing, time_bucket):
    own_rows = latents.shape[0]
    features = latents.shape[1]
    row_count = lax.axis_size("row")
    col_count = lax.axis_size("col")
    total_rows = own_rows * row_count * col_count
    offset = entropic * math.log(total_rows)
    column = lax.axis_index("col")
    row_place = lax.axis_index("row")
    noise_rows = lax.all_gather(noise, "row", axis=0, tiled=True)
    noise_span = noise_rows.shape[0]
    noise_norms = jnp.sum(jnp.square(noise_rows.astype(jnp.float32)), axis=1)
    data_rows = lax.all_gather(latents, "col", axis=0, tiled=True)
    section_norms = jnp.sum(jnp.square(data_rows.astype(jnp.float32)), axis=1)
    products = lax.dot_general(
        data_rows, noise_rows, (((1,), (1,)), ((), ())), preferred_element_type=jnp.float32
    )
    cost = (section_norms[:, None] + noise_norms[None, :] - 2.0 * products) / features
    capacity = 2 * own_rows // col_count
    requests = pairing.reshape(col_count, own_rows)
    wanted = requests // noise_span == column
    block_rank = jnp.cumsum(wanted.astype(jnp.int32), axis=1) - 1
    slot_ids = jnp.arange(capacity)
    chosen = wanted[:, None, :] & (block_rank[:, None, :] == slot_ids[None, :, None])
    local_rows = jnp.sum(jnp.where(chosen, (requests - column * noise_span)[:, None, :], 0), axis=2)
    send_rows = noise_rows[local_rows]
    potential_g = jnp.zeros((noise_span,), jnp.float32)
    potential_f = jnp.zeros((cost.shape[0],), jnp.float32)
    for iteration in range(ITERS):
        potential_f = row_update(cost, potential_g, offset)
        potential_g = column_update(cost, potential_f, offset)
    sent_potential = potential_g[local_rows]
    arrived, arrived_potential = (
        lax.all_to_all(send_rows, "col", split_axis=0, concat_axis=0, tiled=True),
        lax.all_to_all(
            sent_potential.astype(jnp.bfloat16), "col", split_axis=0, concat_axis=0, tiled=True
        ).astype(sent_potential.dtype),
    )
    own_requests = lax.dynamic_slice_in_dim(pairing, column * own_rows, own_rows)
    anchor = own_requests // noise_span
    marker = (anchor[:, None] == jnp.arange(col_count)[None, :]).astype(jnp.int32)
    slot_place = jnp.sum(marker * jnp.cumsum(marker, axis=0), axis=1) - 1
    flat_slot = anchor * capacity + slot_place
    paired = arrived.reshape(col_count * capacity, features)[flat_slot]
    paired_g = arrived_potential.reshape(col_count * capacity)[flat_slot]
    own_f = lax.dynamic_slice_in_dim(potential_f, column * own_rows, own_rows)
    own_g = lax.dynamic_slice_in_dim(potential_g, row_place * own_rows, own_rows)
    data_values = latents.astype(jnp.float32)
    noise_values = paired.astype(jnp.float32)
    pair_cost = jnp.sum(jnp.square(data_values - noise_values), axis=1) / features
    log_weight = (own_f + paired_g - pair_cost) / entropic + math.log(total_rows)
    moment = (time_bucket.astype(jnp.float32) + 0.5) / BUCKETS
    interpolant = ((1.0 - moment)[:, None] * data_values + moment[:, None] * noise_values).astype(
        jnp.bfloat16
    )
    return (own_f, own_g, interpolant, log_weight)


def solution(mesh):
    placed = (P(("row", "col"), None), P(("col", "row"), None), P("row"), P(("row", "col")))
    return jax.shard_map(
        shards,
        mesh=mesh,
        in_specs=placed,
        out_specs=(
            P(("row", "col")),
            P(("col", "row")),
            P(("row", "col"), None),
            P(("row", "col")),
        ),
        check_vma=False,
    )
```

profile of v0, /device:TPU:1, one launch (start us, length us, event | category | flops | bytes accessed | tf_op | source)
XLA Modules:
  0.0 1057.2 jit_solution(5240732509701376048)
XLA Ops:
  13.1 0.8 and_select_fusion
  13.9 31.7 %all-gather.5.cloned.1.call-done = bf16[2048,1024]{1,0:T(8,128)(2,1)} async-done(((bf16[256,1024]{1,0:T(8,128)(2,1)}), bf16[2048,1024]{1,0:T(8,128)(2,1)}) %all-gather.5.cloned.1.call-update) | async-done | bytes 4194320 | tf_op jit(solution)/shard_map/all_gather | solution.py:38
  45.6 6.2 gather_fusion
  51.8 6.7 all-to-all-start
  58.5 0.8 compare_select_fusion.1
  59.3 1.3 broadcast_subtract_fusion.1
  60.6 3.1 multiply_reduce_fusion.1
  63.7 18.3 %all-to-all-done = bf16[16,32,1024]{2,1,0:T(8,128)(2,1)S(1)} async-done(((bf16[16,32,1024]{2,1,0:T(8,128)(2,1)}), bf16[16,32,1024]{2,1,0:T(8,128)(2,1)S(1)}, u32[]{:S(2)}, u32[]{:S(2)}) %all-to-all-start) | async-done | bytes 1048608 | tf_op jit(solution)/shard_map/all_to_all | solution.py:62
  82.0 2.0 gather_fusion.1
  83.9 44.3 %all-gather.3.cloned.1.call-done = bf16[4096,1024]{1,0:T(8,128)(2,1)} async-done(((bf16[256,1024]{1,0:T(8,128)(2,1)}), bf16[4096,1024]{1,0:T(8,128)(2,1)}) %all-gather.3.cloned.1.call-update) | async-done | bytes 8388624 | tf_op jit(solution)/shard_map/all_gather | solution.py:41
  128.3 5.1 multiply_reduce_fusion
  133.4 29.3 %fusion = (f32[4096]{0:T(1024)S(1)}, f32[4096,2048]{1,0:T(8,128)}) fusion(bf16[4096,1024]{1,0:T(8,128)(2,1)} %all-gather.3.cloned.1.call-done, bf16[2048,1024]{1,0:T(8,128)(2,1)} %all-gather.5.cloned.1.call-done, f32[2048]{0:T(1024)S(1)} %multiply_reduce_fusion.1, f32[4096]{0:T(1024)S(1)} %multiply_reduce_fusion), kind=kOutput, calls=%fused_computation.21 | convolution fusion | flops 17238585344 | bytes 46178304 | tf_op jit(solution)/shard_map/dot_general | solution.py:43
  162.7 58.2 %pmax.56 = f32[4096]{0:T(1024)S(1)} all-reduce(f32[4096]{0:T(1024)S(1)} %get-tuple-element.10), channel_id=1, replica_groups=mesh['row'=8,'col'=16] {'col'}, use_global_device_ids=true, to_apply=%region_3.4 | all-reduce | flops 4096 | bytes 32768 | tf_op jit(solution)/shard_map/pmax | solution.py:17
  220.8 14.7 %exponential_reduce_fusion.7 = f32[4096]{0:T(1024)S(1)} fusion(f32[4096,2048]{1,0:T(8,128)} %get-tuple-element.11, f32[4096]{0:T(1024)S(1)} %pmax.56), kind=kLoop, calls=%fused_computation.18 | loop fusion | flops 33550336 | bytes 33587200 | tf_op jit(solution)/shard_map/reduce_sum | solution.py:18
  235.6 56.1 %psum.56 = f32[4096]{0:T(1024)S(1)} all-reduce(f32[4096]{0:T(1024)S(1)} %exponential_reduce_fusion.7), channel_id=1, replica_groups=mesh['row'=8,'col'=16] {'col'}, use_global_device_ids=true, to_apply=%region_5.6 | all-reduce | flops 4096 | bytes 32768 | tf_op jit(solution)/shard_map/psum | solution.py:18
  291.7 13.0 %fusion.1 = f32[2048]{0:T(1024)S(1)} fusion(f32[4096,2048]{1,0:T(8,128)} %get-tuple-element.11, f32[4096]{0:T(1024)S(1)} %multiply_add_fusion.3), kind=kLoop, calls=%fused_computation.22 | loop fusion | flops 25163776 | bytes 33579008 | tf_op jit(solution)/shard_map/reduce_max | solution.py:24
  304.6 40.5 %pmax.57 = f32[2048]{0:T(1024)S(1)} all-reduce(f32[2048]{0:T(1024)S(1)} %fusion.1), channel_id=1, replica_groups=mesh['row'=8,'col'=16] {'row'}, use_global_device_ids=true, to_apply=%region_7.8 | all-reduce | flops 2048 | bytes 16384 | tf_op jit(solution)/shard_map/pmax | solution.py:24
  345.2 14.8 %exponential_reduce_fusion.6 = f32[2048]{0:T(1024)S(1)} fusion(f32[4096,2048]{1,0:T(8,128)} %get-tuple-element.11, f32[2048]{0:T(1024)S(1)} %pmax.57, f32[4096]{0:T(1024)S(1)} %multiply_add_fusion.3), kind=kLoop, calls=%fused_computation.16 | loop fusion | flops 33552384 | bytes 33587200 | tf_op jit(solution)/shard_map/reduce_sum | solution.py:25
  360.0 12.7 %psum.57 = f32[2048]{0:T(1024)S(1)} all-reduce(f32[2048]{0:T(1024)S(1)} %exponential_reduce_fusion.6), channel_id=1, replica_groups=mesh['row'=8,'col'=16] {'row'}, use_global_device_ids=true, to_apply=%region_9.10 | all-reduce | flops 2048 | bytes 16384 | tf_op jit(solution)/shard_map/psum | solution.py:25
  372.7 13.3 %fusion.2 = f32[4096]{0:T(1024)S(1)} fusion(f32[4096,2048]{1,0:T(8,128)} %get-tuple-element.11, f32[2048]{0:T(1024)S(1)} %multiply_add_fusion.7), kind=kLoop, calls=%fused_computation.23 | loop fusion | flops 25161728 | bytes 33579008 | tf_op jit(solution)/shard_map/reduce_max | solution.py:17
  385.9 56.3 %pmax.58 = f32[4096]{0:T(1024)S(1)} all-reduce(f32[4096]{0:T(1024)S(1)} %fusion.2), channel_id=1, replica_groups=mesh['row'=8,'col'=16] {'col'}, use_global_device_ids=true, to_apply=%region_11.12 | all-reduce | flops 4096 | bytes 32768 | tf_op jit(solution)/shard_map/pmax | solution.py:17
  442.2 14.7 %exponential_reduce_fusion.5 = f32[4096]{0:T(1024)S(1)} fusion(f32[4096,2048]{1,0:T(8,128)} %get-tuple-element.11, f32[4096]{0:T(1024)S(1)} %pmax.58, f32[2048]{0:T(1024)S(1)} %multiply_add_fusion.7), kind=kLoop, calls=%fused_computation.14 | loop fusion | flops 33550336 | bytes 33595392 | tf_op jit(solution)/shard_map/reduce_sum | solution.py:18
  457.0 55.8 %psum.58 = f32[4096]{0:T(1024)S(1)} all-reduce(f32[4096]{0:T(1024)S(1)} %exponential_reduce_fusion.5), channel_id=1, replica_groups=mesh['row'=8,'col'=16] {'col'}, use_global_device_ids=true, to_apply=%region_13.14 | all-reduce | flops 4096 | bytes 32768 | tf_op jit(solution)/shard_map/psum | solution.py:18
  512.8 13.0 %fusion.3 = f32[2048]{0:T(1024)S(1)} fusion(f32[4096,2048]{1,0:T(8,128)} %get-tuple-element.11, f32[4096]{0:T(1024)S(1)} %multiply_add_fusion.2), kind=kLoop, calls=%fused_computation.24 | loop fusion | flops 25163776 | bytes 33579008 | tf_op jit(solution)/shard_map/reduce_max | solution.py:24
  525.7 39.7 %pmax.59 = f32[2048]{0:T(1024)S(1)} all-reduce(f32[2048]{0:T(1024)S(1)} %fusion.3), channel_id=1, replica_groups=mesh['row'=8,'col'=16] {'row'}, use_global_device_ids=true, to_apply=%region_15.16 | all-reduce | flops 2048 | bytes 16384 | tf_op jit(solution)/shard_map/pmax | solution.py:24
  565.4 14.8 %exponential_reduce_fusion.4 = f32[2048]{0:T(1024)S(1)} fusion(f32[4096,2048]{1,0:T(8,128)} %get-tuple-element.11, f32[2048]{0:T(1024)S(1)} %pmax.59, f32[4096]{0:T(1024)S(1)} %multiply_add_fusion.2), kind=kLoop, calls=%fused_computation.12 | loop fusion | flops 33552384 | bytes 33587200 | tf_op jit(solution)/shard_map/reduce_sum | solution.py:25
  580.2 12.7 %psum.59 = f32[2048]{0:T(1024)S(1)} all-reduce(f32[2048]{0:T(1024)S(1)} %exponential_reduce_fusion.4), channel_id=1, replica_groups=mesh['row'=8,'col'=16] {'row'}, use_global_device_ids=true, to_apply=%region_17.18 | all-reduce | flops 2048 | bytes 16384 | tf_op jit(solution)/shard_map/psum | solution.py:25
  592.9 13.3 %fusion.4 = f32[4096]{0:T(1024)S(1)} fusion(f32[4096,2048]{1,0:T(8,128)} %get-tuple-element.11, f32[2048]{0:T(1024)S(1)} %multiply_add_fusion.6), kind=kLoop, calls=%fused_computation.25 | loop fusion | flops 25161728 | bytes 33579008 | tf_op jit(solution)/shard_map/reduce_max | solution.py:17
  606.2 56.3 %pmax.60 = f32[4096]{0:T(1024)S(1)} all-reduce(f32[4096]{0:T(1024)S(1)} %fusion.4), channel_id=1, replica_groups=mesh['row'=8,'col'=16] {'col'}, use_global_device_ids=true, to_apply=%region_19.20 | all-reduce | flops 4096 | bytes 32768 | tf_op jit(solution)/shard_map/pmax | solution.py:17
  662.5 14.7 %exponential_reduce_fusion.3 = f32[4096]{0:T(1024)S(1)} fusion(f32[4096,2048]{1,0:T(8,128)} %get-tuple-element.11, f32[4096]{0:T(1024)S(1)} %pmax.60, f32[2048]{0:T(1024)S(1)} %multiply_add_fusion.6), kind=kLoop, calls=%fused_computation.10 | loop fusion | flops 33550336 | bytes 33595392 | tf_op jit(solution)/shard_map/reduce_sum | solution.py:18
  677.2 55.8 %psum.60 = f32[4096]{0:T(1024)S(1)} all-reduce(f32[4096]{0:T(1024)S(1)} %exponential_reduce_fusion.3), channel_id=1, replica_groups=mesh['row'=8,'col'=16] {'col'}, use_global_device_ids=true, to_apply=%region_21.22 | all-reduce | flops 4096 | bytes 32768 | tf_op jit(solution)/shard_map/psum | solution.py:18
  733.0 13.0 %fusion.5 = f32[2048]{0:T(1024)S(1)} fusion(f32[4096,2048]{1,0:T(8,128)} %get-tuple-element.11, f32[4096]{0:T(1024)S(1)} %multiply_add_fusion.1), kind=kLoop, calls=%fused_computation.26 | loop fusion | flops 25163776 | bytes 33579008 | tf_op jit(solution)/shard_map/reduce_max | solution.py:24
  746.0 39.7 %pmax.61 = f32[2048]{0:T(1024)S(1)} all-reduce(f32[2048]{0:T(1024)S(1)} %fusion.5), channel_id=1, replica_groups=mesh['row'=8,'col'=16] {'row'}, use_global_device_ids=true, to_apply=%region_23.24 | all-reduce | flops 2048 | bytes 16384 | tf_op jit(solution)/shard_map/pmax | solution.py:24
  785.6 14.8 %exponential_reduce_fusion.2 = f32[2048]{0:T(1024)S(1)} fusion(f32[4096,2048]{1,0:T(8,128)} %get-tuple-element.11, f32[2048]{0:T(1024)S(1)} %pmax.61, f32[4096]{0:T(1024)S(1)} %multiply_add_fusion.1), kind=kLoop, calls=%fused_computation.8 | loop fusion | flops 33552384 | bytes 33587200 | tf_op jit(solution)/shard_map/reduce_sum | solution.py:25
  800.4 12.7 %psum.61 = f32[2048]{0:T(1024)S(1)} all-reduce(f32[2048]{0:T(1024)S(1)} %exponential_reduce_fusion.2), channel_id=1, replica_groups=mesh['row'=8,'col'=16] {'row'}, use_global_device_ids=true, to_apply=%region_25.26 | all-reduce | flops 2048 | bytes 16384 | tf_op jit(solution)/shard_map/psum | solution.py:25
  813.1 13.3 %fusion.6 = f32[4096]{0:T(1024)S(1)} fusion(f32[4096,2048]{1,0:T(8,128)} %get-tuple-element.11, f32[2048]{0:T(1024)S(1)} %multiply_add_fusion.5), kind=kLoop, calls=%fused_computation.27 | loop fusion | flops 25161728 | bytes 33579008 | tf_op jit(solution)/shard_map/reduce_max | solution.py:17
  826.4 55.9 %pmax.62 = f32[4096]{0:T(1024)S(1)} all-reduce(f32[4096]{0:T(1024)S(1)} %fusion.6), channel_id=1, replica_groups=mesh['row'=8,'col'=16] {'col'}, use_global_device_ids=true, to_apply=%region_27.28 | all-reduce | flops 4096 | bytes 32768 | tf_op jit(solution)/shard_map/pmax | solution.py:17
  882.3 14.8 %exponential_reduce_fusion.1 = f32[4096]{0:T(1024)S(1)} fusion(f32[4096,2048]{1,0:T(8,128)} %get-tuple-element.11, f32[4096]{0:T(1024)S(1)} %pmax.62, f32[2048]{0:T(1024)S(1)} %multiply_add_fusion.5), kind=kLoop, calls=%fused_computation.6 | loop fusion | flops 33550336 | bytes 33595392 | tf_op jit(solution)/shard_map/reduce_sum | solution.py:18
  897.1 55.6 %psum.62 = f32[4096]{0:T(1024)S(1)} all-reduce(f32[4096]{0:T(1024)S(1)} %exponential_reduce_fusion.1), channel_id=1, replica_groups=mesh['row'=8,'col'=16] {'col'}, use_global_device_ids=true, to_apply=%region_29.30 | all-reduce | flops 4096 | bytes 32768 | tf_op jit(solution)/shard_map/psum | solution.py:18
  952.8 13.0 %fusion.7 = f32[2048]{0:T(1024)S(1)} fusion(f32[4096,2048]{1,0:T(8,128)} %get-tuple-element.11, f32[4096]{0:T(1024)S(1)} %multiply_add_fusion), kind=kLoop, calls=%fused_computation.28 | loop fusion | flops 25163776 | bytes 33579008 | tf_op jit(solution)/shard_map/reduce_max | solution.py:24
  965.9 40.4 %pmax.63 = f32[2048]{0:T(1024)S(1)} all-reduce(f32[2048]{0:T(1024)S(1)} %fusion.7), channel_id=1, replica_groups=mesh['row'=8,'col'=16] {'row'}, use_global_device_ids=true, to_apply=%region_31.32 | all-reduce | flops 2048 | bytes 16384 | tf_op jit(solution)/shard_map/pmax | solution.py:24
  1006.3 14.8 %exponential_reduce_fusion = f32[2048]{0:T(1024)S(1)} fusion(f32[4096,2048]{1,0:T(8,128)} %get-tuple-element.11, f32[2048]{0:T(1024)S(1)} %pmax.63, f32[4096]{0:T(1024)S(1)} %multiply_add_fusion), kind=kLoop, calls=%fused_computation.4 | loop fusion | flops 33552384 | bytes 33587200 | tf_op jit(solution)/shard_map/reduce_sum | solution.py:25
  1021.1 12.7 %psum.63 = f32[2048]{0:T(1024)S(1)} all-reduce(f32[2048]{0:T(1024)S(1)} %exponential_reduce_fusion), channel_id=1, replica_groups=mesh['row'=8,'col'=16] {'row'}, use_global_device_ids=true, to_apply=%region_33.34 | all-reduce | flops 2048 | bytes 16384 | tf_op jit(solution)/shard_map/psum | solution.py:25
  1033.8 3.1 gather_fusion.2
  1037.7 3.5 all-to-all-start.1
  1041.2 1.3 fusion.9
  1043.2 4.4 all-to-all-done.1
  1047.6 2.1 gather_fusion.3
  (52 shorter events, 8.1 us)
Async XLA Ops:
  7.2 38.4 %all-gather.5.cloned.1.call-start = ((), (), s32[]{:S(2)}) async-start(), calls=%async_computation.3 | async-start | bytes 4718592 | tf_op jit(solution)/shard_map/all_gather | solution.py:38
  7.9 120.4 %all-gather.3.cloned.1.call-start = ((), (), s32[]{:S(2)}) async-start(), calls=%async_computation.2 | async-start | bytes 8912896 | tf_op jit(solution)/shard_map/all_gather | solution.py:41
  13.9 37.9 %copy-start.2 = (s32[1024]{0:T(1024)}, s32[1024]{0:T(1024)S(1)}, u32[]{:S(2)}) copy-start(s32[1024]{0:T(1024)S(1)} %pad_clamp_fusion.1) | copy-start | bytes 12292
  51.8 30.2 %all-to-all-start = ((bf16[16,32,1024]{2,1,0:T(8,128)(2,1)}), bf16[16,32,1024]{2,1,0:T(8,128)(2,1)S(1)}, u32[]{:S(2)}, u32[]{:S(2)}) async-start(bf16[16,32,1024]{2,1,0:T(8,128)(2,1)} %bitcast.2), calls=%async_computation | async-start | bytes 2097152 | tf_op jit(solution)/shard_map/all_to_all | solution.py:62
  59.3 103.3 %copy-start.4 = (s32[1024]{0:T(1024)}, s32[1024]{0:T(1024)S(1)}, u32[]{:S(2)}) copy-start(s32[1024]{0:T(1024)S(1)} %pad_clamp_fusion) | copy-start | bytes 12292
  952.8 81.0 %copy-start.3 = (s32[1024]{0:T(1024)S(1)}, s32[1024]{0:T(1024)}, u32[]{:S(2)}) copy-start(s32[1024]{0:T(1024)} %copy-done.2) | copy-start | bytes 12292
  952.8 88.4 %copy-start = (bf16[256,1024]{1,0:T(8,128)(2,1)S(1)}, bf16[256,1024]{1,0:T(8,128)(2,1)}, u32[]{:S(2)}) copy-start(bf16[256,1024]{1,0:T(8,128)(2,1)} %gather_fusion.1) | copy-start | bytes 1572868
  952.8 88.4 %copy-start.1 = (bf16[256,1024]{1,0:T(8,128)(2,1)S(1)}, bf16[256,1024]{1,0:T(8,128)(2,1)}, u32[]{:S(2)}) copy-start(bf16[256,1024]{1,0:T(8,128)(2,1)} %param.4) | copy-start | bytes 1572868
  952.8 88.4 %copy-start.5 = (f32[256]{0:T(256)S(1)}, f32[256]{0:T(256)}, u32[]{:S(2)}) copy-start(f32[256]{0:T(256)} %get-tuple-element.8) | copy-start | bytes 3076
  952.8 88.4 %copy-start.6 = (f32[256]{0:T(256)S(1)}, f32[256]{0:T(256)}, u32[]{:S(2)}) copy-start(f32[256]{0:T(256)} %get-tuple-element.9) | copy-start | bytes 3076
  1037.7 9.8 all-to-all-start.1
Sparse Core Ops, SparseCore 0:
  9.7 35.8 all-gather.4
  47.7 80.5 all-gather.2
where the time goes:
time: 1060 us
  blocking collectives  661 us (62%)
  other arithmetic  226 us (21%)
  waiting for transfers between devices  100 us (9%)
  matrix products  29.3 us (3%)
  local copies, waits for them, and re-layouts  16 us (2%)
  between operations  14.4 us (1%)
    pmax x4, blocking collectives, row_update(): peak = lax.pmax(jnp.max(scores, axis=1), 'col')  227 us
    psum x4, blocking collectives, row_update(): running = lax.psum(jnp.sum(jnp.exp(scores - peak[:, None]), axis=1), 'col')  223 us
    pmax x4, blocking collectives, column_update(): peak = lax.pmax(jnp.max(scores, axis=0), 'row')  160 us
    reduce_sum x4, other arithmetic, column_update(): running = lax.psum(jnp.sum(jnp.exp(scores - peak[None, :]), axis=0), 'row')  59.2 us
    reduce_sum x4, other arithmetic, row_update(): running = lax.psum(jnp.sum(jnp.exp(scores - peak[:, None]), axis=1), 'col')  59 us
    reduce_max x4, other arithmetic, column_update(): peak = lax.pmax(jnp.max(scores, axis=0), 'row')  51.9 us
    psum x4, blocking collectives, column_update(): running = lax.psum(jnp.sum(jnp.exp(scores - peak[None, :]), axis=0), 'row')  50.7 us
    all_gather x1, waiting for transfers between devices, shards(): data_rows = lax.all_gather(latents, 'col', axis=0, tiled=True)  44.3 us
  transfers between devices with their start and end apart: 4, of which 4 were waited for; matrix products, arithmetic and copies ran while one was open for 2% of the time, Pallas kernels for 0%

commit v1 on v0

v1 whole, which is shorter than its diff:
```python
import functools
import math

import jax
import jax.numpy as jnp
from jax import lax
from jax.experimental import pallas as pl
from jax.experimental.pallas import tpu as pltpu
from jax.sharding import PartitionSpec as P

ITERS = 4
BUCKETS = 1000
MESH = pl.DeviceIdType.MESH
LOW = 2.0**-40
HIGH = 2.0**40
F32 = jnp.float32
BF16 = jnp.bfloat16

entropic = 0.1


def row_update(cost, potential, offset):
    scores = (potential[None, :] - cost) / entropic
    peak = lax.pmax(jnp.max(scores, axis=1), "col")
    running = lax.psum(jnp.sum(jnp.exp(scores - peak[:, None]), axis=1), "col")
    return -entropic * (peak + jnp.log(running)) - offset


def column_update(cost, potential, offset):
    scores = (potential[:, None] - cost) / entropic
    peak = lax.pmax(jnp.max(scores, axis=0), "row")
    running = lax.psum(jnp.sum(jnp.exp(scores - peak[None, :]), axis=0), "row")
    return -entropic * (peak + jnp.log(running)) - offset


def log_domain(latents, noise, pairing):
    own_rows, features = latents.shape
    col_count = lax.axis_size("col")
    total_rows = own_rows * lax.axis_size("row") * col_count
    offset = entropic * math.log(total_rows)
    column = lax.axis_index("col")
    row_place = lax.axis_index("row")
    noise_rows = lax.all_gather(noise, "row", axis=0, tiled=True)
    noise_span = noise_rows.shape[0]
    noise_norms = jnp.sum(jnp.square(noise_rows.astype(F32)), axis=1)
    data_rows = lax.all_gather(latents, "col", axis=0, tiled=True)
    section_norms = jnp.sum(jnp.square(data_rows.astype(F32)), axis=1)
    products = lax.dot_general(
        data_rows, noise_rows, (((1,), (1,)), ((), ())), preferred_element_type=F32
    )
    cost = (section_norms[:, None] + noise_norms[None, :] - 2.0 * products) / features
    potential_g = jnp.zeros((noise_span,), F32)
    potential_f = jnp.zeros((cost.shape[0],), F32)
    for iteration in range(ITERS):
        potential_f = row_update(cost, potential_g, offset)
        potential_g = column_update(cost, potential_f, offset)
    own_f = lax.dynamic_slice_in_dim(potential_f, column * own_rows, own_rows)
    own_g = lax.dynamic_slice_in_dim(potential_g, row_place * own_rows, own_rows)
    all_g = lax.all_gather(potential_g, "col", axis=0, tiled=True)
    own_requests = lax.dynamic_slice_in_dim(pairing, column * own_rows, own_rows)
    return own_f, own_g, all_g[own_requests]


def dot_nt(a, b):
    return lax.dot_general(a, b, (((1,), (1,)), ((), ())), preferred_element_type=F32)


def dot_nn(a, b):
    return lax.dot_general(a, b, (((1,), (0,)), ((), ())), preferred_element_type=F32)


def three_parts(v):
    hi = v.astype(BF16)
    rest = v - hi.astype(F32)
    mid = rest.astype(BF16)
    low = (rest - mid.astype(F32)).astype(BF16)
    return hi, mid, low


def turn_to_lanes(v):
    n = v.shape[0]
    parts = [
        jnp.sum(jnp.transpose(v[q * 128 : (q + 1) * 128, :]), axis=0, keepdims=True)
        for q in range(n // 128)
    ]
    return parts[0] if len(parts) == 1 else jnp.concatenate(parts, axis=1)


def spread_rows(v):
    return jnp.transpose(jnp.broadcast_to(v, (128, 128)))


def kernel(
    n_row, n_col, features, total_rows,
    lat, noi, req, bucket,
    out_f, out_g, out_w, out_c, out_bad, out_i,
    x_buf, y_buf, e_buf, s_buf, norm_y, wide, pick, send_rows, got_rows,
    f_got, g_got, pg_got, peak, scale, tops, sums, rank,
    own_sem, x_send, x_recv, y_send, y_recv, f_send, f_recv, g_send, g_recv,
    p_send, p_recv, q_send, q_recv,
):
    rows = 256
    span = n_row * rows
    row = lax.axis_index("row")
    col = lax.axis_index("col")
    log2e = math.log2(math.e)
    unit = log2e / (features * entropic)

    def col_peer(k):
        return {"col": lax.rem(col + k, n_col)}

    def row_peer(k):
        return {"row": lax.rem(row + k, n_row)}

    barrier = pltpu.get_barrier_semaphore()

    def greet_col(k, _):
        pl.semaphore_signal(barrier, inc=1, device_id=col_peer(k), device_id_type=MESH)
        return 0

    def greet_row(k, _):
        pl.semaphore_signal(barrier, inc=1, device_id=row_peer(k), device_id_type=MESH)
        return 0

    lax.fori_loop(1, n_col, greet_col, 0)
    lax.fori_loop(1, n_row, greet_row, 0)
    own_x = pltpu.make_async_copy(lat, x_buf.at[col], own_sem.at[0])
    own_y = pltpu.make_async_copy(noi, y_buf.at[row], own_sem.at[1])
    own_x.start()
    own_y.start()
    pl.semaphore_wait(barrier, n_col + n_row - 2)

    def x_copy(k):
        return pltpu.make_async_remote_copy(
            src_ref=lat, dst_ref=x_buf.at[col], send_sem=x_send.at[k], recv_sem=x_recv.at[k],
            device_id=col_peer(k), device_id_type=MESH,
        )

    def y_copy(k):
        return pltpu.make_async_remote_copy(
            src_ref=noi, dst_ref=y_buf.at[row], send_sem=y_send.at[k], recv_sem=y_recv.at[k],
            device_id=row_peer(k), device_id_type=MESH,
        )

    def f_copy(it, k):
        return pltpu.make_async_remote_copy(
            src_ref=f_got.at[it, col], dst_ref=f_got.at[it, col],
            send_sem=f_send.at[it, k], recv_sem=f_recv.at[it, k],
            device_id=col_peer(k), device_id_type=MESH,
        )

    def g_copy(it, k):
        return pltpu.make_async_remote_copy(
            src_ref=g_got.at[it, row], dst_ref=g_got.at[it, row],
            send_sem=g_send.at[it, k], recv_sem=g_recv.at[it, k],
            device_id=row_peer(k), device_id_type=MESH,
        )

    def p_copy(k):
        return pltpu.make_async_remote_copy(
            src_ref=send_rows.at[lax.rem(col + k, n_col)], dst_ref=got_rows.at[col],
            send_sem=p_send.at[k], recv_sem=p_recv.at[k],
            device_id=col_peer(k), device_id_type=MESH,
        )

    def q_copy(k):
        return pltpu.make_async_remote_copy(
            src_ref=pg_got.at[n_col + lax.rem(col + k, n_col) // 4], dst_ref=pg_got.at[col],
            send_sem=q_send.at[k], recv_sem=q_recv.at[k],
            device_id=col_peer(k), device_id_type=MESH,
        )

    def each(n, act):
        def step(k, _):
            act(k)
            return 0

        lax.fori_loop(1, n, step, 0)

    each(n_row, lambda k: y_copy(k).start())
    each(n_col, lambda k: x_copy(k).start())

    requests = req[...]
    before = (
        lax.broadcasted_iota(jnp.int32, (rows, rows), 0)
        < lax.broadcasted_iota(jnp.int32, (rows, rows), 1)
    ).astype(F32).astype(BF16)
    wanted = ((requests // span) == col).astype(F32)
    place = dot_nn(wanted.astype(BF16), before)
    rank[0:n_col, :] = jnp.where(wanted > 0.0, place, -1.0)
    rank[n_col : 2 * n_col, :] = (requests - col * span + 1).astype(F32)

    slots = lax.broadcasted_iota(jnp.int32, (32, rows), 0).astype(F32)
    places = lax.broadcasted_iota(jnp.int32, (32, span), 1).astype(F32) + 1.0

    def choose(d, _):
        chosen = rank[pl.ds(d, 1), :] == slots
        index = jnp.sum(jnp.where(chosen, rank[pl.ds(n_col + d, 1), :], 0.0), axis=1, keepdims=True)
        pick[pl.ds(pl.multiple_of(d * 32, 32), 32), :] = (places == index).astype(F32).astype(BF16)
        return 0

    lax.fori_loop(0, n_col, choose, 0)

    own_y.wait()
    each(n_row, lambda k: y_copy(k).wait_recv())

    def norms(r, _):
        v = y_buf[r].astype(F32)
        n = jnp.sum(v * v, axis=1, keepdims=True) * unit
        norm_y[pl.ds(pl.multiple_of(r * rows, rows), rows), :] = jnp.broadcast_to(n, (rows, 128))
        return 0

    lax.fori_loop(0, n_row, norms, 0)

    def fill(q, _):
        at = pl.multiple_of(q * 128, 128)
        total = jnp.zeros((128, features), F32)
        for r in range(n_row):
            total = total + dot_nn(pick[pl.ds(at, 128), r * rows : (r + 1) * rows], y_buf[r])
        send_rows[pl.ds(q * 4, 4)] = total.astype(BF16).reshape(4, 32, features)
        return 0

    lax.fori_loop(0, n_col // 4, fill, 0)
    got_rows[col] = send_rows[col]

    def scores(slot, c, r):
        at = pl.multiple_of(r * rows, rows)
        norm = norm_y[pl.ds(at, rows), :]
        t = dot_nt(y_buf[r], x_buf[c]) * (2.0 * unit) - jnp.concatenate([norm, norm], axis=1)
        s_buf[slot, pl.ds(at, rows), :] = t
        tops[slot] = jnp.maximum(tops[slot], jnp.max(t.reshape(rows // 8, 8, rows), axis=0))

    def powers(slot, c, r):
        at = pl.multiple_of(r * rows, rows)
        v = jnp.exp2(s_buf[slot, pl.ds(at, rows), :] - peak[pl.ds(c, 1), :])
        e_buf[c, pl.ds(at, rows), :] = v
        sums[slot] = sums[slot] + jnp.sum(v.reshape(rows // 8, 8, rows), axis=0)

    def opened(slot):
        tops[slot] = jnp.full((8, rows), -3.0e38, F32)
        sums[slot] = jnp.zeros((8, rows), F32)

    def topped(slot, c):
        peak[pl.ds(c, 1), :] = jnp.max(tops[slot], axis=0, keepdims=True)

    def closed(slot, c):
        total = jnp.sum(sums[slot], axis=0, keepdims=True)
        f_got[0, col, pl.ds(c, 1), :] = peak[pl.ds(c, 1), :] + jnp.log2(total)

    def block_of(k):
        return lax.rem(col + n_col - k, n_col)

    own_x.wait()
    opened(0)
    lax.fori_loop(0, n_row, lambda r, _: (scores(0, col, r), 0)[1], 0)
    topped(0, col)

    def block(k, _):
        x_copy(k).wait_recv()
        slot = lax.rem(k, 2)
        c = block_of(k)
        p = block_of(k - 1)
        opened(slot)

        def both(r, _):
            scores(slot, c, r)
            powers(1 - slot, p, r)
            return 0

        lax.fori_loop(0, n_row, both, 0)
        topped(slot, c)
        closed(1 - slot, p)
        return 0

    lax.fori_loop(1, n_col, block, 0)
    last = (n_col - 1) % 2
    lax.fori_loop(0, n_row, lambda r, _: (powers(last, block_of(n_col - 1), r), 0)[1], 0)
    closed(last, block_of(n_col - 1))

    def in_range(v):
        return (v >= LOW) & (v <= HIGH)

    def column_pass(it):
        def body(q, _):
            at = pl.multiple_of(q * 32, 32)
            total = jnp.zeros((32, rows), F32)
            for c in range(n_col):
                total = total + e_buf[c, pl.ds(at, 32), :] * scale[c : c + 1, :]
            wide[pl.ds(at, 32), :] = total[:, :128] + total[:, 128:]
            return 0

        lax.fori_loop(0, span // 32, body, 0)
        for r in range(n_row):
            g_got[it, row, r : r + 1, :] = turn_to_lanes(wide[r * rows : (r + 1) * rows, :])

    def row_pass(it):
        for q in range(n_col // 4):

            def body(j, acc):
                at = pl.multiple_of(j * 64, 64)
                b = wide[pl.ds(at, 64), :]
                b = jnp.concatenate([b, b], axis=1)
                return tuple(
                    acc[i] + jnp.sum((e_buf[q * 4 + i, pl.ds(at, 64), :] * b).reshape(8, 8, rows), axis=0)
                    for i in range(4)
                )

            acc = lax.fori_loop(0, span // 64, body, tuple(jnp.zeros((8, rows), F32) for _ in range(4)))
            for i in range(4):
                c = q * 4 + i
                f_got[it, col, c : c + 1, :] = jnp.sum(acc[i], axis=0, keepdims=True) * scale[n_col + c : n_col + c + 1, :]

    def summed(ref, it, n):
        total = ref[it, 0]
        for d in range(1, n):
            total = total + ref[it, d]
        return total

    own_lse = None
    own_p = None
    big_q = None
    for it in range(ITERS):
        if it > 0:
            row_pass(it)
        each(n_col, lambda k: f_copy(it, k).start())
        each(n_col, lambda k: f_copy(it, k).wait_recv())
        if it == 0:
            top = f_got[0, 0]
            for d in range(1, n_col):
                top = jnp.maximum(top, f_got[0, d])
            total = jnp.zeros_like(top)
            for d in range(n_col):
                total = total + jnp.exp2(f_got[0, d] - top)
            lse = top + jnp.log2(total)
            rank[0:n_col, :] = lse
            weight = jnp.exp2(peak[...] - lse)
            scale[n_col : 2 * n_col, :] = weight
            scale[0:n_col, :] = weight
        else:
            total = summed(f_got, it, n_col)
            a = jnp.where(in_range(total), 1.0 / total, jnp.nan)
            scale[0:n_col, :] = a * scale[n_col : 2 * n_col, :]
            if it == ITERS - 1:
                rank[n_col : 2 * n_col, :] = total
        column_pass(it)
        each(n_row, lambda k: g_copy(it, k).start())
        if it == 0:
            each(n_col, lambda k: p_copy(k).start())
        if it == ITERS - 1:
            each(n_col, lambda k: p_copy(k).wait_recv())
            mine = req[pl.ds(col, 1), :]
            anchor = mine // span
            marker = lax.broadcasted_iota(jnp.int32, (n_col, rows), 0) == anchor
            marked = marker.astype(F32)
            spot = jnp.sum(marked * dot_nn(marked.astype(BF16), before), axis=0, keepdims=True)
            flat = anchor.astype(F32) * 32.0 + spot
            tick = (bucket[...].astype(F32) + 0.5) / BUCKETS
            lanes = lax.broadcasted_iota(jnp.int32, (128, 32 * n_col), 1).astype(F32)
            costs = []
            squares = []
            for h in range(2):
                flat_h = spread_rows(flat[:, h * 128 : (h + 1) * 128])
                take = (lanes == flat_h[:, :1]).astype(F32).astype(BF16)
                paired = dot_nn(take, got_rows[...].reshape(32 * n_col, features))
                data = x_buf[col, h * 128 : (h + 1) * 128, :].astype(F32)
                t = spread_rows(tick[:, h * 128 : (h + 1) * 128])[:, :1]
                out_i[h * 128 : (h + 1) * 128, :] = ((1.0 - t) * data + t * paired).astype(BF16)
                diff = data - paired
                cost = diff * diff
                square = data * data
                fold_c = cost[:, :128]
                fold_s = square[:, :128]
                for q in range(1, features // 128):
                    fold_c = fold_c + cost[:, q * 128 : (q + 1) * 128]
                    fold_s = fold_s + square[:, q * 128 : (q + 1) * 128]
                costs.append(turn_to_lanes(fold_c))
                squares.append(turn_to_lanes(fold_s))
            pair_cost = jnp.concatenate(costs, axis=1) / features
            norm_x = jnp.concatenate(squares, axis=1) / features
        each(n_row, lambda k: g_copy(it, k).wait_recv())
        big_q = summed(g_got, it, n_row)
        if it < ITERS - 1:
            b = jnp.where(in_range(big_q), 1.0 / big_q, jnp.nan)
            for r in range(n_row):
                for h in range(2):
                    at = r * rows + h * 128
                    wide[at : at + 128, :] = spread_rows(b[r : r + 1, h * 128 : (h + 1) * 128])

    fine = jnp.min(jnp.where(in_range(big_q), 1.0, 0.0), axis=(0, 1), keepdims=True)
    g = jnp.where(fine > 0.0, -entropic * jnp.log(big_q), jnp.nan)
    chosen = [jnp.zeros((8, 32 * n_col), F32)]
    for part in three_parts(g):
        for r in range(n_row):
            one = jnp.broadcast_to(part[r : r + 1, :], (8, rows))
            chosen[0] = chosen[0] + dot_nt(one, pick[:, r * rows : (r + 1) * rows])
    for q in range(n_col // 4):
        pg_got[n_col + q] = chosen[0][:1, q * 128 : (q + 1) * 128]
    each(n_col, lambda k: q_copy(k).start())
    pg_got[col] = pg_got[n_col + col // 4]
    log_total = math.log(total_rows)
    lse = rank[pl.ds(col, 1), :]
    own_p = rank[pl.ds(n_col + col, 1), :]
    f = norm_x - entropic * (lse / log2e + jnp.log(own_p) + log_total)
    out_f[...] = f
    rank[0:n_row, :] = g
    out_g[...] = rank[pl.ds(row, 1), :]
    offset = lax.rem(col, 4) * 32
    grab = (
        lax.broadcasted_iota(jnp.int32, (128, rows), 0).astype(F32) == spot + offset.astype(F32)
    ).astype(F32).astype(BF16)
    each(n_col, lambda k: q_copy(k).wait_recv())
    arrived = jnp.concatenate([pg_got[d] for d in range(n_col)], axis=0)
    paired_g = jnp.zeros((n_col, rows), F32)
    for part in three_parts(arrived):
        paired_g = paired_g + dot_nn(part, grab)
    paired_g = jnp.sum(jnp.where(marker, paired_g, 0.0), axis=0, keepdims=True)
    out_c[...] = pair_cost
    out_w[...] = (f + paired_g - pair_cost) / entropic + log_total
    out_bad[...] = jnp.broadcast_to(
        jnp.max(jnp.where(arrived == arrived, 0.0, 1.0), axis=(0, 1), keepdims=True), (1, 128)
    )

    each(n_row, lambda k: y_copy(k).wait_send())
    each(n_col, lambda k: x_copy(k).wait_send())
    each(n_col, lambda k: p_copy(k).wait_send())
    each(n_col, lambda k: q_copy(k).wait_send())
    for it in range(ITERS):
        each(n_col, lambda k: f_copy(it, k).wait_send())
        each(n_row, lambda k: g_copy(it, k).wait_send())


def shards(latents, noise, pairing, time_bucket):
    own_rows, features = latents.shape
    n_row = lax.axis_size("row")
    n_col = lax.axis_size("col")
    total_rows = own_rows * n_row * n_col
    span = own_rows * n_row
    vmem = pl.BlockSpec(memory_space=pltpu.VMEM)
    hbm = pl.BlockSpec(memory_space=pl.ANY)
    line = jax.ShapeDtypeStruct((1, own_rows), F32)
    dma = pltpu.SemaphoreType.DMA
    f, g, w, pair_cost, bad, interpolant = pl.pallas_call(
        functools.partial(kernel, n_row, n_col, features, total_rows),
        out_shape=(
            line, line, line, line,
            jax.ShapeDtypeStruct((1, 128), F32),
            jax.ShapeDtypeStruct((own_rows, features), BF16),
        ),
        in_specs=[hbm, hbm, vmem, vmem],
        out_specs=(vmem,) * 6,
        scratch_shapes=[
            pltpu.VMEM((n_col, own_rows, features), BF16),
            pltpu.VMEM((n_row, own_rows, features), BF16),
            pltpu.VMEM((n_col, span, own_rows), F32),
            pltpu.VMEM((2, span, own_rows), F32),
            pltpu.VMEM((span, 128), F32),
            pltpu.VMEM((span, 128), F32),
            pltpu.VMEM((32 * n_col, span), BF16),
            pltpu.VMEM((n_col, 32, features), BF16),
            pltpu.VMEM((n_col, 32, features), BF16),
            pltpu.VMEM((ITERS, n_col, n_col, own_rows), F32),
            pltpu.VMEM((ITERS, n_row, n_row, own_rows), F32),
            pltpu.VMEM((n_col + n_col // 4, 1, 128), F32),
            pltpu.VMEM((n_col, own_rows), F32),
            pltpu.VMEM((2 * n_col, own_rows), F32),
            pltpu.VMEM((2, 8, own_rows), F32),
            pltpu.VMEM((2, 8, own_rows), F32),
            pltpu.VMEM((2 * n_col, own_rows), F32),
            dma((2,)),
            dma((n_col,)), dma((n_col,)),
            dma((n_row,)), dma((n_row,)),
            dma((ITERS, n_col)), dma((ITERS, n_col)),
            dma((ITERS, n_row)), dma((ITERS, n_row)),
            dma((n_col,)), dma((n_col,)),
            dma((n_col,)), dma((n_col,)),
        ],
        compiler_params=pltpu.CompilerParams(
            collective_id=0, has_side_effects=True, vmem_limit_bytes=62 * 1024 * 1024
        ),
        name="pairing_plan",
    )(latents, noise, pairing.reshape(n_col, own_rows), time_bucket.reshape(1, own_rows))
    f, g, w, pair_cost = (v.reshape(own_rows) for v in (f, g, w, pair_cost))

    def again():
        exact_f, exact_g, paired_g = log_domain(latents, noise, pairing)
        log_weight = (exact_f + paired_g - pair_cost) / entropic + math.log(total_rows)
        return exact_f, exact_g, log_weight

    f, g, w = lax.cond(bad[0, 0] > 0.0, again, lambda: (f, g, w))
    return f, g, interpolant, w


def solution(mesh):
    placed = (P(("row", "col"), None), P(("col", "row"), None), P("row"), P(("row", "col")))
    return jax.shard_map(
        shards,
        mesh=mesh,
        in_specs=placed,
        out_specs=(
            P(("row", "col")),
            P(("col", "row")),
            P(("row", "col"), None),
            P(("row", "col")),
        ),
        check_vma=False,
    )
```

time: 1060 us -> 265 us (0.25)
  blocking collectives: 661 us -> 0 us
  Pallas kernels: 0 us -> 244 us
  other arithmetic: 226 us -> 0 us
  waiting for transfers between devices: 100 us -> 0 us
  matrix products: 29.3 us -> 0 us
    pmax x8 -> x0, blocking collectives: 387 us -> none  [the longest x4 227 us: row_update(): peak = lax.pmax(jnp.max(scores, axis=1), 'col')]
    psum x8 -> x0, blocking collectives: 274 us -> none  [the longest x4 223 us: row_update(): running = lax.psum(jnp.sum(jnp.exp(scores - peak[:, None]), axis=1), 'col')]
    pallas_call x0 -> x1, Pallas kernels: none -> 244 us  [shards(): pl.pallas_call(functools.partial(kernel, n_row, n_col, features, total_ro...]
    reduce_sum x12 -> x0, other arithmetic: 127 us -> none  [the longest x4 59.2 us: column_update(): running = lax.psum(jnp.sum(jnp.exp(scores - peak[None, :]), axis=0), 'row')]
    reduce_max x7 -> x0, other arithmetic: 91.7 us -> none  [the longest x4 51.9 us: column_update(): peak = lax.pmax(jnp.max(scores, axis=0), 'row')]
    all_gather x2 -> x0, waiting for transfers between devices: 76 us -> none  [the longest x1 44.3 us: shards(): data_rows = lax.all_gather(latents, 'col', axis=0, tiled=True)]
    dot_general x1 -> x0, matrix products: 29.3 us -> none  [shards(): lax.dot_general(data_rows, noise_rows, (((1,), (1,)), ((), ())), preferre...]
    all_to_all x2 -> x0, waiting for transfers between devices: 22.7 us -> none  [the longest x1 18.3 us: shards(): lax.all_to_all(send_rows, 'col', split_axis=0, concat_axis=0, tiled=True)]
  transfers between devices with their start and end apart: 4 -> 0, of which waited for: 4 -> 0; matrix products, arithmetic and copies ran while one was open for 2% -> 0% of each run, Pallas kernels for 0% -> 0%
where the time goes in v1:
time: 265 us
  Pallas kernels  244 us (92%)
  between operations  14.7 us (6%)
  local copies, waits for them, and re-layouts  5.8 us (2%)
    pallas_call x1, Pallas kernels, shards(): pl.pallas_call(functools.partial(kernel, n_row, n_col, features, total_ro...  244 us

profile of v1, /device:TPU:1, one launch (start us, length us, event | category | flops | bytes accessed | tf_op | source)
XLA Modules:
  0.0 265.0 jit_solution(12067449794244116453)
XLA Ops:
  7.2 1.3 reshape.50.req
  8.5 244.3 %pairing_plan.1 = (f32[1,256]{1,0:T(1,128)}, f32[1,256]{1,0:T(1,128)}, f32[1,256]{1,0:T(1,128)}, f32[1,256]{1,0:T(1,128)}, f32[1,128]{1,0:T(1,128)}, /*index=5*/bf16[256,1024]{1,0:T(8,128)(2,1)}) custom-call(bf16[256,1024]{1,0:T(8,128)(2,1)} %lat.1, bf16[256,1024]{1,0:T(8,128)(2,1)} %noi.1, s32[16,256]{1,0:T(8,128)} %reshape.50.req, s32[1,256]{1,0:T(1,128)} %bitcast.9), custom_call_target="tpu_custom_call" | custom-call | tf_op jit(solution)/shard_map/pairing_plan/pallas_call | solution.py:442
  253.5 0.0 copy-start
  253.5 0.2 conditional.1
  253.7 1.2 copy.18
  255.0 1.2 copy.19
  256.2 0.0 copy-done
  256.2 0.8 copy.20
  257.0 1.2 copy.21
Async XLA Ops:
  253.5 2.7 %copy-start = (bf16[256,1024]{1,0:T(8,128)(2,1)S(1)}, bf16[256,1024]{1,0:T(8,128)(2,1)}, u32[]{:S(2)}) copy-start(bf16[256,1024]{1,0:T(8,128)(2,1)} %get-tuple-element.69) | copy-start | bytes 1572868

commit v2 on v1

--- a/solution.py
+++ b/solution.py
@@ -95,7 +95,7 @@
     lat, noi, req, bucket,
     out_f, out_g, out_w, out_c, out_bad, out_i,
     x_buf, y_buf, e_buf, s_buf, norm_y, wide, pick, send_rows, got_rows,
-    f_got, g_got, pg_got, peak, scale, tops, sums, rank,
+    f_got, g_got, pg_got, peak, scale, rank,
     own_sem, x_send, x_recv, y_send, y_recv, f_send, f_recv, g_send, g_recv,
     p_send, p_recv, q_send, q_recv,
 ):
@@ -130,17 +130,90 @@
     own_y.start()
     pl.semaphore_wait(barrier, n_col + n_row - 2)
 
-    def x_copy(k):
+    z, x = col // 4, lax.rem(col, 4)
+    y, core = row // 2, lax.rem(row, 2)
+
+    def col_at(dz, dx):
+        return lax.rem(z + (dz + 8), 4) * 4 + lax.rem(x + (dx + 8), 4)
+
+    steps = {"x+": (0, 1), "x-": (0, -1), "z+": (1, 0), "z-": (-1, 0)}
+    half = rows // 2
+    quarter = rows // 4
+    x_moves = {}
+    for way in steps:
+        first = way[1] == "+"
+        back = -1 if first else 1
+        if way[0] == "x":
+            x_moves[way, "A"] = (0, 0, 0, half)
+            x_moves[way, "fA"] = (0, back, 0 if first else quarter, quarter)
+            x_moves[way, "B"] = (0, 0, half, half)
+            for d in (-1, 1, 2):
+                x_moves[way, "B", d] = (d, 0, half, half)
+            for d in (0, -1, 1, 2):
+                x_moves[way, "fB", d] = (d, back, half if first else half + quarter, quarter)
+        else:
+            x_moves[way, "B"] = (0, 0, half, half)
+            x_moves[way, "fB"] = (back, 0, half if first else half + quarter, quarter)
+            x_moves[way, "A"] = (0, 0, 0, half)
+            for d in (-1, 1, 2):
+                x_moves[way, "A", d] = (0, d, 0, half)
+            for d in (0, -1, 1, 2):
+                x_moves[way, "fA", d] = (back, d, 0 if first else quarter, quarter)
+    x_index = {move: i for i, move in enumerate(x_moves)}
+
+    def x_copy(move, arriving):
+        way = steps[move[0]]
+        dz, dx, start, count = x_moves[move]
+        i = x_index[move]
+        shift = way if arriving else (0, 0)
+        place = x_buf.at[col_at(dz - shift[0], dx - shift[1]), pl.ds(start, count)]
+        source = place
+        if not arriving and (dz, dx) == (0, 0):
+            source = lat.at[pl.ds(start, count)]
         return pltpu.make_async_remote_copy(
-            src_ref=lat, dst_ref=x_buf.at[col], send_sem=x_send.at[k], recv_sem=x_recv.at[k],
-            device_id=col_peer(k), device_id_type=MESH,
+            src_ref=source, dst_ref=place, send_sem=x_send.at[i], recv_sem=x_recv.at[i],
+            device_id={"col": col_at(*way)}, device_id_type=MESH,
         )
 
-    def y_copy(k):
+    def x_start(*moves):
+        for move in moves:
+            x_copy(move, False).start()
+
+    def x_wait(*moves):
+        for move in moves:
+            x_copy(move, True).wait_recv()
+
+    def row_at(dy, other):
+        return lax.rem(y + (dy + 8), 4) * 2 + (1 - core if other else core)
+
+    y_moves = {
+        "+0": (1, 0, 0, half), "-1": (-1, 0, half, half),
+        "+1": (1, 0, half, half), "-0": (-1, 0, 0, half),
+        "+f": (1, -1, 0, half), "-f": (-1, 1, half, half),
+        "s": (0, 0, 0, rows), "sm": (0, -1, 0, rows), "sp": (0, 1, 0, rows),
+        "s0": (0, 2, 0, half), "s1": (0, 2, half, half),
+    }
+    y_index = {move: i for i, move in enumerate(y_moves)}
+
+    def y_copy(move, arriving):
+        way, dy, start, count = y_moves[move]
+        i = y_index[move]
+        place = y_buf.at[row_at(dy - (way if arriving else 0), arriving and way == 0), pl.ds(start, count)]
+        source = place
+        if not arriving and dy == 0:
+            source = noi.at[pl.ds(start, count)]
         return pltpu.make_async_remote_copy(
-            src_ref=noi, dst_ref=y_buf.at[row], send_sem=y_send.at[k], recv_sem=y_recv.at[k],
-            device_id=row_peer(k), device_id_type=MESH,
+            src_ref=source, dst_ref=place, send_sem=y_send.at[i], recv_sem=y_recv.at[i],
+            device_id={"row": row_at(way, way == 0)}, device_id_type=MESH,
         )
+
+    def y_start(*moves):
+        for move in moves:
+            y_copy(move, False).start()
+
+    def y_wait(*moves):
+        for move in moves:
+            y_copy(move, True).wait_recv()
 
     def f_copy(it, k):
         return pltpu.make_async_remote_copy(
@@ -171,14 +244,13 @@
         )
 
     def each(n, act):
-        def step(k, _):
+        for k in range(1, n):
             act(k)
-            return 0
-
-        lax.fori_loop(1, n, step, 0)
-
-    each(n_row, lambda k: y_copy(k).start())
-    each(n_col, lambda k: x_copy(k).start())
+
+    y_start("+0", "-1", "s")
+    x_start(("x+", "A"), ("x-", "A"), ("z+", "B"), ("z-", "B"))
+    y_start("+1", "-0")
+    x_start(("x+", "B"), ("x-", "B"), ("z+", "A"), ("z-", "A"))
 
     requests = req[...]
     before = (
@@ -201,8 +273,39 @@
 
     lax.fori_loop(0, n_col, choose, 0)
 
+    own_x.wait()
     own_y.wait()
-    each(n_row, lambda k: y_copy(k).wait_recv())
+    y_wait("+0")
+    y_start("+f")
+    y_wait("-1")
+    y_start("-f")
+    x_wait(("x+", "A"))
+    x_start(("x+", "fA"), ("z+", "A", -1), ("z-", "A", -1))
+    x_wait(("x-", "A"))
+    x_start(("x-", "fA"), ("z+", "A", 1), ("z-", "A", 1))
+    x_wait(("z+", "B"))
+    x_start(("z+", "fB"), ("x+", "B", -1), ("x-", "B", -1))
+    x_wait(("z-", "B"))
+    x_start(("z-", "fB"), ("x+", "B", 1), ("x-", "B", 1))
+    y_wait("+1")
+    y_start("sm")
+    y_wait("-0")
+    y_start("sp")
+    for way in ("x+", "x-"):
+        x_wait((way, "B"))
+        x_start((way, "fB", 0))
+    for way in ("z+", "z-"):
+        x_wait((way, "A"))
+        x_start((way, "fA", 0))
+    x_wait(("x+", "fA"), ("x-", "fA"))
+    x_start(("z+", "A", 2), ("z-", "A", 2))
+    x_wait(("z+", "fB"), ("z-", "fB"))
+    x_start(("x+", "B", 2), ("x-", "B", 2))
+    y_wait("+f")
+    y_start("s0")
+    y_wait("-f")
+    y_start("s1")
+    y_wait("s", "sm", "sp", "s0", "s1")
 
     def norms(r, _):
         v = y_buf[r].astype(F32)
@@ -212,103 +315,93 @@
 
     lax.fori_loop(0, n_row, norms, 0)
 
-    def fill(q, _):
-        at = pl.multiple_of(q * 128, 128)
-        total = jnp.zeros((128, features), F32)
-        for r in range(n_row):
-            total = total + dot_nn(pick[pl.ds(at, 128), r * rows : (r + 1) * rows], y_buf[r])
-        send_rows[pl.ds(q * 4, 4)] = total.astype(BF16).reshape(4, 32, features)
-        return 0
-
-    lax.fori_loop(0, n_col // 4, fill, 0)
-    got_rows[col] = send_rows[col]
-
-    def scores(slot, c, r):
-        at = pl.multiple_of(r * rows, rows)
-        norm = norm_y[pl.ds(at, rows), :]
-        t = dot_nt(y_buf[r], x_buf[c]) * (2.0 * unit) - jnp.concatenate([norm, norm], axis=1)
-        s_buf[slot, pl.ds(at, rows), :] = t
-        tops[slot] = jnp.maximum(tops[slot], jnp.max(t.reshape(rows // 8, 8, rows), axis=0))
-
-    def powers(slot, c, r):
-        at = pl.multiple_of(r * rows, rows)
-        v = jnp.exp2(s_buf[slot, pl.ds(at, rows), :] - peak[pl.ds(c, 1), :])
-        e_buf[c, pl.ds(at, rows), :] = v
-        sums[slot] = sums[slot] + jnp.sum(v.reshape(rows // 8, 8, rows), axis=0)
-
-    def opened(slot):
-        tops[slot] = jnp.full((8, rows), -3.0e38, F32)
-        sums[slot] = jnp.zeros((8, rows), F32)
-
-    def topped(slot, c):
-        peak[pl.ds(c, 1), :] = jnp.max(tops[slot], axis=0, keepdims=True)
-
-    def closed(slot, c):
-        total = jnp.sum(sums[slot], axis=0, keepdims=True)
-        f_got[0, col, pl.ds(c, 1), :] = peak[pl.ds(c, 1), :] + jnp.log2(total)
-
-    def block_of(k):
-        return lax.rem(col + n_col - k, n_col)
-
-    own_x.wait()
-    opened(0)
-    lax.fori_loop(0, n_row, lambda r, _: (scores(0, col, r), 0)[1], 0)
-    topped(0, col)
-
-    def block(k, _):
-        x_copy(k).wait_recv()
-        slot = lax.rem(k, 2)
-        c = block_of(k)
-        p = block_of(k - 1)
-        opened(slot)
-
-        def both(r, _):
-            scores(slot, c, r)
-            powers(1 - slot, p, r)
+    def block(c):
+        latent = x_buf[c]
+        norm = norm_y[...]
+        t = dot_nt(y_buf[...].reshape(span, features), latent) * (2.0 * unit)
+        t = t - jnp.concatenate([norm, norm], axis=1)
+        s_buf[...] = t
+        top = jnp.max(jnp.max(t.reshape(span // 8, 8, rows), axis=0), axis=0, keepdims=True)
+        peak[pl.ds(c, 1), :] = top
+
+        def powers(r, total):
+            at = pl.multiple_of(r * 512, 512)
+            v = jnp.exp2(s_buf[pl.ds(at, 512), :] - top)
+            e_buf[c, pl.ds(at, 512), :] = v
+            return total + jnp.sum(v.reshape(64, 8, rows), axis=0)
+
+        total = lax.fori_loop(0, span // 512, powers, jnp.zeros((8, rows), F32))
+        f_got[0, col, pl.ds(c, 1), :] = top + jnp.log2(jnp.sum(total, axis=0, keepdims=True))
+
+    near = (-1, 1)
+    blocks = ((0, 0), (0, -1), (0, 1), (-1, 0), (1, 0), (-1, -1), (-1, 1), (1, -1), (1, 1),
+              (0, 2), (2, 0), (-1, 2), (1, 2), (2, -1), (2, 1), (2, 2))
+
+    def some_blocks(first, last):
+        def step(k, _):
+            dz = jnp.int32(0)
+            dx = jnp.int32(0)
+            for i in range(first, last):
+                dz = jnp.where(k == i, blocks[i][0], dz)
+                dx = jnp.where(k == i, blocks[i][1], dx)
+            block(lax.rem(z + dz + 8, 4) * 4 + lax.rem(x + dx + 8, 4))
             return 0
 
-        lax.fori_loop(0, n_row, both, 0)
-        topped(slot, c)
-        closed(1 - slot, p)
-        return 0
-
-    lax.fori_loop(1, n_col, block, 0)
-    last = (n_col - 1) % 2
-    lax.fori_loop(0, n_row, lambda r, _: (powers(last, block_of(n_col - 1), r), 0)[1], 0)
-    closed(last, block_of(n_col - 1))
+        lax.fori_loop(first, last, step, 0)
+
+    some_blocks(0, 4)
+    for d in near:
+        for way in ("x+", "x-"):
+            x_wait((way, "B", d))
+            x_start((way, "fB", d))
+        for way in ("z+", "z-"):
+            x_wait((way, "A", d))
+            x_start((way, "fA", d))
+    some_blocks(4, 8)
+    for way in ("x+", "x-"):
+        x_wait((way, "B", 2))
+        x_start((way, "fB", 2))
+    for way in ("z+", "z-"):
+        x_wait((way, "A", 2))
+        x_start((way, "fA", 2))
+    some_blocks(8, 9)
+    x_wait(("x+", "fB", 0), ("x-", "fB", 0), ("z+", "fA", 0), ("z-", "fA", 0))
+    some_blocks(9, 11)
+    for d in near:
+        x_wait(("x+", "fB", d), ("x-", "fB", d), ("z+", "fA", d), ("z-", "fA", d))
+    some_blocks(11, 15)
+    x_wait(("x+", "fB", 2), ("x-", "fB", 2), ("z+", "fA", 2), ("z-", "fA", 2))
+    some_blocks(15, 16)
 
     def in_range(v):
         return (v >= LOW) & (v <= HIGH)
 
     def column_pass(it):
         def body(q, _):
-            at = pl.multiple_of(q * 32, 32)
-            total = jnp.zeros((32, rows), F32)
+            at = pl.multiple_of(q * 256, 256)
+            total = jnp.zeros((256, rows), F32)
             for c in range(n_col):
-                total = total + e_buf[c, pl.ds(at, 32), :] * scale[c : c + 1, :]
-            wide[pl.ds(at, 32), :] = total[:, :128] + total[:, 128:]
+                total = total + e_buf[c, pl.ds(at, 256), :] * scale[c : c + 1, :]
+            wide[pl.ds(at, 256), :] = total[:, :128] + total[:, 128:]
             return 0
 
-        lax.fori_loop(0, span // 32, body, 0)
+        lax.fori_loop(0, span // 256, body, 0)
         for r in range(n_row):
             g_got[it, row, r : r + 1, :] = turn_to_lanes(wide[r * rows : (r + 1) * rows, :])
 
     def row_pass(it):
-        for q in range(n_col // 4):
-
-            def body(j, acc):
-                at = pl.multiple_of(j * 64, 64)
-                b = wide[pl.ds(at, 64), :]
-                b = jnp.concatenate([b, b], axis=1)
-                return tuple(
-                    acc[i] + jnp.sum((e_buf[q * 4 + i, pl.ds(at, 64), :] * b).reshape(8, 8, rows), axis=0)
-                    for i in range(4)
-                )
-
-            acc = lax.fori_loop(0, span // 64, body, tuple(jnp.zeros((8, rows), F32) for _ in range(4)))
-            for i in range(4):
-                c = q * 4 + i
-                f_got[it, col, c : c + 1, :] = jnp.sum(acc[i], axis=0, keepdims=True) * scale[n_col + c : n_col + c + 1, :]
+        def body(j, acc):
+            at = pl.multiple_of(j * 128, 128)
+            b = wide[pl.ds(at, 128), :]
+            b = jnp.concatenate([b, b], axis=1)
+            return tuple(
+                acc[c] + jnp.sum((e_buf[c, pl.ds(at, 128), :] * b).reshape(16, 8, rows), axis=0)
+                for c in range(n_col)
+            )
+
+        acc = lax.fori_loop(0, span // 128, body, tuple(jnp.zeros((8, rows), F32) for _ in range(n_col)))
+        for c in range(n_col):
+            f_got[it, col, c : c + 1, :] = jnp.sum(acc[c], axis=0, keepdims=True) * scale[n_col + c : n_col + c + 1, :]
 
     def summed(ref, it, n):
         total = ref[it, 0]
@@ -316,13 +409,25 @@
             total = total + ref[it, d]
         return total
 
-    own_lse = None
-    own_p = None
+    def prepare():
+        def fill(q, _):
+            at = pl.multiple_of(q * 128, 128)
+            total = jnp.zeros((128, features), F32)
+            for r in range(n_row):
+                total = total + dot_nn(pick[pl.ds(at, 128), r * rows : (r + 1) * rows], y_buf[r])
+            send_rows[pl.ds(q * 4, 4)] = total.astype(BF16).reshape(4, 32, features)
+            return 0
+
+        lax.fori_loop(0, n_col // 4, fill, 0)
+        got_rows[col] = send_rows[col]
+
     big_q = None
     for it in range(ITERS):
         if it > 0:
             row_pass(it)
         each(n_col, lambda k: f_copy(it, k).start())
+        if it == 0:
+            prepare()
         each(n_col, lambda k: f_copy(it, k).wait_recv())
         if it == 0:
             top = f_got[0, 0]
@@ -344,8 +449,9 @@
                 rank[n_col : 2 * n_col, :] = total
         column_pass(it)
         each(n_row, lambda k: g_copy(it, k).start())
-        if it == 0:
-            each(n_col, lambda k: p_copy(k).start())
+        if it < ITERS - 1:
+            for k in range(1 + 5 * it, 6 + 5 * it):
+                p_copy(k).start()
         if it == ITERS - 1:
             each(n_col, lambda k: p_copy(k).wait_recv())
             mine = req[pl.ds(col, 1), :]
@@ -420,8 +526,10 @@
         jnp.max(jnp.where(arrived == arrived, 0.0, 1.0), axis=(0, 1), keepdims=True), (1, 128)
     )
 
-    each(n_row, lambda k: y_copy(k).wait_send())
-    each(n_col, lambda k: x_copy(k).wait_send())
+    for move in y_moves:
+        y_copy(move, False).wait_send()
+    for move in x_moves:
+        x_copy(move, False).wait_send()
     each(n_col, lambda k: p_copy(k).wait_send())
     each(n_col, lambda k: q_copy(k).wait_send())
     for it in range(ITERS):
@@ -452,7 +560,7 @@
             pltpu.VMEM((n_col, own_rows, features), BF16),
             pltpu.VMEM((n_row, own_rows, features), BF16),
             pltpu.VMEM((n_col, span, own_rows), F32),
-            pltpu.VMEM((2, span, own_rows), F32),
+            pltpu.VMEM((span, own_rows), F32),
             pltpu.VMEM((span, 128), F32),
             pltpu.VMEM((span, 128), F32),
             pltpu.VMEM((32 * n_col, span), BF16),
@@ -463,12 +571,10 @@
             pltpu.VMEM((n_col + n_col // 4, 1, 128), F32),
             pltpu.VMEM((n_col, own_rows), F32),
             pltpu.VMEM((2 * n_col, own_rows), F32),
-            pltpu.VMEM((2, 8, own_rows), F32),
-            pltpu.VMEM((2, 8, own_rows), F32),
             pltpu.VMEM((2 * n_col, own_rows), F32),
             dma((2,)),
-            dma((n_col,)), dma((n_col,)),
-            dma((n_row,)), dma((n_row,)),
+            dma((40,)), dma((40,)),
+            dma((11,)), dma((11,)),
             dma((ITERS, n_col)), dma((ITERS, n_col)),
             dma((ITERS, n_row)), dma((ITERS, n_row)),
             dma((n_col,)), dma((n_col,)),

time: 265 us -> 155 us (0.58)
  Pallas kernels: 244 us -> 134 us
    pallas_call x1, Pallas kernels: 244 us -> 134 us  [shards(): pl.pallas_call(functools.partial(kernel, n_row, n_col, features, total_ro...]
where the time goes in v2:
time: 155 us
  Pallas kernels  134 us (86%)
  between operations  14.7 us (9%)
  local copies, waits for them, and re-layouts  5.8 us (4%)
    pallas_call x1, Pallas kernels, shards(): pl.pallas_call(functools.partial(kernel, n_row, n_col, features, total_ro...  134 us
    unnamed x6, local copies, waits for them, and re-layouts  4.48 us

profile of v2, /device:TPU:1, one launch (start us, length us, event | category | flops | bytes accessed | tf_op | source)
XLA Modules:
  0.0 154.8 jit_solution(18059214606839329850)
XLA Ops:
  7.2 1.3 reshape.50.req
  8.5 134.0 %pairing_plan.1 = (f32[1,256]{1,0:T(1,128)}, f32[1,256]{1,0:T(1,128)}, f32[1,256]{1,0:T(1,128)}, f32[1,256]{1,0:T(1,128)}, f32[1,128]{1,0:T(1,128)}, /*index=5*/bf16[256,1024]{1,0:T(8,128)(2,1)}) custom-call(bf16[256,1024]{1,0:T(8,128)(2,1)} %lat.1, bf16[256,1024]{1,0:T(8,128)(2,1)} %noi.1, s32[16,256]{1,0:T(8,128)} %reshape.50.req, s32[1,256]{1,0:T(1,128)} %bitcast.9), custom_call_target="tpu_custom_call" | custom-call | tf_op jit(solution)/shard_map/pairing_plan/pallas_call | solution.py:550
  143.2 0.0 copy-start
  143.2 0.3 conditional.1
  143.4 1.2 copy.18
  144.7 1.2 copy.19
  145.9 0.0 copy-done
  145.9 0.8 copy.20
  146.7 1.2 copy.21
Async XLA Ops:
  143.2 2.8 %copy-start = (bf16[256,1024]{1,0:T(8,128)(2,1)S(1)}, bf16[256,1024]{1,0:T(8,128)(2,1)}, u32[]{:S(2)}) copy-start(bf16[256,1024]{1,0:T(8,128)(2,1)} %get-tuple-element.69) | copy-start | bytes 1572868

commit v3 on v2

--- a/solution.py
+++ b/solution.py
@@ -19,17 +19,48 @@
 entropic = 0.1
 
 
+def next_one(value, axis):
+    count = lax.axis_size(axis)
+    return lax.ppermute(value, axis, [(i, (i + 1) % count) for i in range(count)])
+
+
+def over(value, axis, join):
+    def step(_, carry):
+        passing, total = carry
+        passing = next_one(passing, axis)
+        return passing, join(total, passing)
+
+    return lax.fori_loop(1, lax.axis_size(axis), step, (value, value))[1]
+
+
+def whole(value, axis):
+    count = lax.axis_size(axis)
+    size = value.shape[0]
+    place = lax.axis_index(axis)
+
+    def put(out, part, index):
+        return lax.dynamic_update_slice_in_dim(out, part, index * size, 0)
+
+    def step(k, carry):
+        passing, out = carry
+        passing = next_one(passing, axis)
+        return passing, put(out, passing, lax.rem(place + count - k, count))
+
+    out = put(jnp.zeros((count * size,) + value.shape[1:], value.dtype), value, place)
+    return lax.fori_loop(1, count, step, (value, out))[1]
+
+
 def row_update(cost, potential, offset):
     scores = (potential[None, :] - cost) / entropic
-    peak = lax.pmax(jnp.max(scores, axis=1), "col")
-    running = lax.psum(jnp.sum(jnp.exp(scores - peak[:, None]), axis=1), "col")
+    peak = over(jnp.max(scores, axis=1), "col", jnp.maximum)
+    running = over(jnp.sum(jnp.exp(scores - peak[:, None]), axis=1), "col", jnp.add)
     return -entropic * (peak + jnp.log(running)) - offset
 
 
 def column_update(cost, potential, offset):
     scores = (potential[:, None] - cost) / entropic
-    peak = lax.pmax(jnp.max(scores, axis=0), "row")
-    running = lax.psum(jnp.sum(jnp.exp(scores - peak[None, :]), axis=0), "row")
+    peak = over(jnp.max(scores, axis=0), "row", jnp.maximum)
+    running = over(jnp.sum(jnp.exp(scores - peak[None, :]), axis=0), "row", jnp.add)
     return -entropic * (peak + jnp.log(running)) - offset
 
 
@@ -40,10 +71,10 @@
     offset = entropic * math.log(total_rows)
     column = lax.axis_index("col")
     row_place = lax.axis_index("row")
-    noise_rows = lax.all_gather(noise, "row", axis=0, tiled=True)
+    noise_rows = whole(noise, "row")
     noise_span = noise_rows.shape[0]
     noise_norms = jnp.sum(jnp.square(noise_rows.astype(F32)), axis=1)
-    data_rows = lax.all_gather(latents, "col", axis=0, tiled=True)
+    data_rows = whole(latents, "col")
     section_norms = jnp.sum(jnp.square(data_rows.astype(F32)), axis=1)
     products = lax.dot_general(
         data_rows, noise_rows, (((1,), (1,)), ((), ())), preferred_element_type=F32
@@ -51,12 +82,14 @@
     cost = (section_norms[:, None] + noise_norms[None, :] - 2.0 * products) / features
     potential_g = jnp.zeros((noise_span,), F32)
     potential_f = jnp.zeros((cost.shape[0],), F32)
-    for iteration in range(ITERS):
-        potential_f = row_update(cost, potential_g, offset)
-        potential_g = column_update(cost, potential_f, offset)
+    def iterate(_, potentials):
+        updated = row_update(cost, potentials[1], offset)
+        return updated, column_update(cost, updated, offset)
+
+    potential_f, potential_g = lax.fori_loop(0, ITERS, iterate, (potential_f, potential_g))
     own_f = lax.dynamic_slice_in_dim(potential_f, column * own_rows, own_rows)
     own_g = lax.dynamic_slice_in_dim(potential_g, row_place * own_rows, own_rows)
-    all_g = lax.all_gather(potential_g, "col", axis=0, tiled=True)
+    all_g = whole(potential_g, "col")
     own_requests = lax.dynamic_slice_in_dim(pairing, column * own_rows, own_rows)
     return own_f, own_g, all_g[own_requests]
 
@@ -95,8 +128,8 @@
     lat, noi, req, bucket,
     out_f, out_g, out_w, out_c, out_bad, out_i,
     x_buf, y_buf, e_buf, s_buf, norm_y, wide, pick, send_rows, got_rows,
-    f_got, g_got, pg_got, peak, scale, rank,
-    own_sem, x_send, x_recv, y_send, y_recv, f_send, f_recv, g_send, g_recv,
+    fx_got, fz_got, g_got, pg_got, peak, scale, rank, asked,
+    own_sem, x_send, x_recv, y_send, y_recv, fx_send, fx_recv, fz_send, fz_recv, g_send, g_recv,
     p_send, p_recv, q_send, q_recv,
 ):
     rows = 256
@@ -215,11 +248,18 @@
         for move in moves:
             y_copy(move, True).wait_recv()
 
-    def f_copy(it, k):
+    def fx_copy(it, k):
         return pltpu.make_async_remote_copy(
-            src_ref=f_got.at[it, col], dst_ref=f_got.at[it, col],
-            send_sem=f_send.at[it, k], recv_sem=f_recv.at[it, k],
-            device_id=col_peer(k), device_id_type=MESH,
+            src_ref=fx_got.at[it, x], dst_ref=fx_got.at[it, x],
+            send_sem=fx_send.at[it, k], recv_sem=fx_recv.at[it, k],
+            device_id={"col": col_at(0, k)}, device_id_type=MESH,
+        )
+
+    def fz_copy(it, k):
+        return pltpu.make_async_remote_copy(
+            src_ref=fz_got.at[it, z], dst_ref=fz_got.at[it, z],
+            send_sem=fz_send.at[it, k], recv_sem=fz_recv.at[it, k],
+            device_id={"col": col_at(k, 0)}, device_id_type=MESH,
         )
 
     def g_copy(it, k):
@@ -252,7 +292,9 @@
     y_start("+1", "-0")
     x_start(("x+", "B"), ("x-", "B"), ("z+", "A"), ("z-", "A"))
 
-    requests = req[...]
+    for c in range(n_col):
+        asked[c : c + 1, :] = jnp.concatenate([req[2 * c : 2 * c + 1, :], req[2 * c + 1 : 2 * c + 2, :]], axis=1)
+    requests = asked[...]
     before = (
         lax.broadcasted_iota(jnp.int32, (rows, rows), 0)
         < lax.broadcasted_iota(jnp.int32, (rows, rows), 1)
@@ -331,7 +373,7 @@
             return total + jnp.sum(v.reshape(64, 8, rows), axis=0)
 
         total = lax.fori_loop(0, span // 512, powers, jnp.zeros((8, rows), F32))
-        f_got[0, col, pl.ds(c, 1), :] = top + jnp.log2(jnp.sum(total, axis=0, keepdims=True))
+        fx_got[0, x, pl.ds(c, 1), :] = top + jnp.log2(jnp.sum(total, axis=0, keepdims=True))
 
     near = (-1, 1)
     blocks = ((0, 0), (0, -1), (0, 1), (-1, 0), (1, 0), (-1, -1), (-1, 1), (1, -1), (1, 1),
@@ -401,7 +443,14 @@
 
         acc = lax.fori_loop(0, span // 128, body, tuple(jnp.zeros((8, rows), F32) for _ in range(n_col)))
         for c in range(n_col):
-            f_got[it, col, c : c + 1, :] = jnp.sum(acc[c], axis=0, keepdims=True) * scale[n_col + c : n_col + c + 1, :]
+            fx_got[it, x, c : c + 1, :] = jnp.sum(acc[c], axis=0, keepdims=True) * scale[n_col + c : n_col + c + 1, :]
+
+    def log_sum(ref, it):
+        top = jnp.maximum(jnp.maximum(ref[it, 0], ref[it, 1]), jnp.maximum(ref[it, 2], ref[it, 3]))
+        total = jnp.exp2(ref[it, 0] - top)
+        for d in range(1, 4):
+            total = total + jnp.exp2(ref[it, d] - top)
+        return top + jnp.log2(total)
 
     def summed(ref, it, n):
         total = ref[it, 0]
@@ -425,24 +474,21 @@
     for it in range(ITERS):
         if it > 0:
             row_pass(it)
-        each(n_col, lambda k: f_copy(it, k).start())
+        each(4, lambda k: fx_copy(it, k).start())
         if it == 0:
             prepare()
-        each(n_col, lambda k: f_copy(it, k).wait_recv())
+        each(4, lambda k: fx_copy(it, k).wait_recv())
+        fz_got[it, z] = log_sum(fx_got, it) if it == 0 else summed(fx_got, it, 4)
+        each(4, lambda k: fz_copy(it, k).start())
+        each(4, lambda k: fz_copy(it, k).wait_recv())
         if it == 0:
-            top = f_got[0, 0]
-            for d in range(1, n_col):
-                top = jnp.maximum(top, f_got[0, d])
-            total = jnp.zeros_like(top)
-            for d in range(n_col):
-                total = total + jnp.exp2(f_got[0, d] - top)
-            lse = top + jnp.log2(total)
+            lse = log_sum(fz_got, it)
             rank[0:n_col, :] = lse
             weight = jnp.exp2(peak[...] - lse)
             scale[n_col : 2 * n_col, :] = weight
             scale[0:n_col, :] = weight
         else:
-            total = summed(f_got, it, n_col)
+            total = summed(fz_got, it, 4)
             a = jnp.where(in_range(total), 1.0 / total, jnp.nan)
             scale[0:n_col, :] = a * scale[n_col : 2 * n_col, :]
             if it == ITERS - 1:
@@ -454,7 +500,7 @@
                 p_copy(k).start()
         if it == ITERS - 1:
             each(n_col, lambda k: p_copy(k).wait_recv())
-            mine = req[pl.ds(col, 1), :]
+            mine = asked[pl.ds(col, 1), :]
             anchor = mine // span
             marker = lax.broadcasted_iota(jnp.int32, (n_col, rows), 0) == anchor
             marked = marker.astype(F32)
@@ -493,7 +539,7 @@
                     wide[at : at + 128, :] = spread_rows(b[r : r + 1, h * 128 : (h + 1) * 128])
 
     fine = jnp.min(jnp.where(in_range(big_q), 1.0, 0.0), axis=(0, 1), keepdims=True)
-    g = jnp.where(fine > 0.0, -entropic * jnp.log(big_q), jnp.nan)
+    g = jnp.where(fine > 0.0, jnp.log(big_q), jnp.nan)
     chosen = [jnp.zeros((8, 32 * n_col), F32)]
     for part in three_parts(g):
         for r in range(n_row):
@@ -506,8 +552,8 @@
     log_total = math.log(total_rows)
     lse = rank[pl.ds(col, 1), :]
     own_p = rank[pl.ds(n_col + col, 1), :]
-    f = norm_x - entropic * (lse / log2e + jnp.log(own_p) + log_total)
-    out_f[...] = f
+    f_scaled = lse / log2e + jnp.log(own_p) + log_total - norm_x / entropic
+    out_f[...] = f_scaled
     rank[0:n_row, :] = g
     out_g[...] = rank[pl.ds(row, 1), :]
     offset = lax.rem(col, 4) * 32
@@ -521,10 +567,8 @@
         paired_g = paired_g + dot_nn(part, grab)
     paired_g = jnp.sum(jnp.where(marker, paired_g, 0.0), axis=0, keepdims=True)
     out_c[...] = pair_cost
-    out_w[...] = (f + paired_g - pair_cost) / entropic + log_total
-    out_bad[...] = jnp.broadcast_to(
-        jnp.max(jnp.where(arrived == arrived, 0.0, 1.0), axis=(0, 1), keepdims=True), (1, 128)
-    )
+    out_w[...] = f_scaled + paired_g + pair_cost / entropic - log_total
+    out_bad[0, 0] = jnp.max(jnp.where(arrived == arrived, 0.0, 1.0)).astype(jnp.int32)
 
     for move in y_moves:
         y_copy(move, False).wait_send()
@@ -533,7 +577,8 @@
     each(n_col, lambda k: p_copy(k).wait_send())
     each(n_col, lambda k: q_copy(k).wait_send())
     for it in range(ITERS):
-        each(n_col, lambda k: f_copy(it, k).wait_send())
+        each(4, lambda k: fx_copy(it, k).wait_send())
+        each(4, lambda k: fz_copy(it, k).wait_send())
         each(n_row, lambda k: g_copy(it, k).wait_send())
 
 
@@ -551,11 +596,11 @@
         functools.partial(kernel, n_row, n_col, features, total_rows),
         out_shape=(
             line, line, line, line,
-            jax.ShapeDtypeStruct((1, 128), F32),
+            jax.ShapeDtypeStruct((1, 1), jnp.int32),
             jax.ShapeDtypeStruct((own_rows, features), BF16),
         ),
         in_specs=[hbm, hbm, vmem, vmem],
-        out_specs=(vmem,) * 6,
+        out_specs=(vmem,) * 4 + (pl.BlockSpec(memory_space=pltpu.SMEM), vmem),
         scratch_shapes=[
             pltpu.VMEM((n_col, own_rows, features), BF16),
             pltpu.VMEM((n_row, own_rows, features), BF16),
@@ -566,16 +611,19 @@
             pltpu.VMEM((32 * n_col, span), BF16),
             pltpu.VMEM((n_col, 32, features), BF16),
             pltpu.VMEM((n_col, 32, features), BF16),
-            pltpu.VMEM((ITERS, n_col, n_col, own_rows), F32),
+            pltpu.VMEM((ITERS, 4, n_col, own_rows), F32),
+            pltpu.VMEM((ITERS, 4, n_col, own_rows), F32),
             pltpu.VMEM((ITERS, n_row, n_row, own_rows), F32),
             pltpu.VMEM((n_col + n_col // 4, 1, 128), F32),
             pltpu.VMEM((n_col, own_rows), F32),
             pltpu.VMEM((2 * n_col, own_rows), F32),
             pltpu.VMEM((2 * n_col, own_rows), F32),
+            pltpu.VMEM((n_col, own_rows), jnp.int32),
             dma((2,)),
             dma((40,)), dma((40,)),
             dma((11,)), dma((11,)),
-            dma((ITERS, n_col)), dma((ITERS, n_col)),
+            dma((ITERS, 4)), dma((ITERS, 4)),
+            dma((ITERS, 4)), dma((ITERS, 4)),
             dma((ITERS, n_row)), dma((ITERS, n_row)),
             dma((n_col,)), dma((n_col,)),
             dma((n_col,)), dma((n_col,)),
@@ -584,16 +632,15 @@
             collective_id=0, has_side_effects=True, vmem_limit_bytes=62 * 1024 * 1024
         ),
         name="pairing_plan",
-    )(latents, noise, pairing.reshape(n_col, own_rows), time_bucket.reshape(1, own_rows))
-    f, g, w, pair_cost = (v.reshape(own_rows) for v in (f, g, w, pair_cost))
-
+    )(latents, noise, pairing.reshape(2 * n_col, own_rows // 2), time_bucket.reshape(1, own_rows))
     def again():
         exact_f, exact_g, paired_g = log_domain(latents, noise, pairing)
-        log_weight = (exact_f + paired_g - pair_cost) / entropic + math.log(total_rows)
-        return exact_f, exact_g, log_weight
-
-    f, g, w = lax.cond(bad[0, 0] > 0.0, again, lambda: (f, g, w))
-    return f, g, interpolant, w
+        log_weight = (exact_f + paired_g - pair_cost.reshape(own_rows)) / entropic + math.log(total_rows)
+        return tuple(v.reshape(1, own_rows) for v in (exact_f / -entropic, exact_g / -entropic, -log_weight))
+
+    f, g, w = lax.cond(bad[0, 0] > 0, again, lambda: (f, g, w))
+    f, g, w = (v.reshape(own_rows) for v in (f, g, w))
+    return f * -entropic, g * -entropic, interpolant, -w
 
 
 def solution(mesh):

time: 155 us -> 143 us (0.923)
  between operations: 14.7 us -> 1.35 us
  Pallas kernels: 134 us -> 137 us
  local copies, waits for them, and re-layouts: 5.8 us -> 2.89 us
    pallas_call x1, Pallas kernels: 134 us -> 137 us  [shards(): pl.pallas_call(functools.partial(kernel, n_row, n_col, features, total_ro...]
    unnamed x6 -> x7, local copies, waits for them, and re-layouts: 4.48 us -> 2.89 us
where the time goes in v3:
time: 143 us
  Pallas kernels  137 us (96%)
  local copies, waits for them, and re-layouts  2.89 us (2%)
    pallas_call x1, Pallas kernels, shards(): pl.pallas_call(functools.partial(kernel, n_row, n_col, features, total_ro...  137 us
    unnamed x7, local copies, waits for them, and re-layouts  2.89 us

profile of v3, /device:TPU:1, one launch (start us, length us, event | category | flops | bytes accessed | tf_op | source)
XLA Modules:
  0.0 143.0 jit_solution(7026704722958017587)
XLA Ops:
  0.6 1.0 copy.98.lat
  1.7 1.0 copy.99.noi
  2.7 137.2 %pairing_plan.1 = (f32[1,256]{1,0:T(1,128)}, f32[1,256]{1,0:T(1,128)}, f32[1,256]{1,0:T(1,128)S(1)}, f32[1,256]{1,0:T(1,128)}, s32[1,1]{1,0:T(1,128)}, /*index=5*/bf16[256,1024]{1,0:T(8,128)(2,1)}) custom-call(bf16[256,1024]{1,0:T(8,128)(2,1)S(1)} %copy.98.lat, bf16[256,1024]{1,0:T(8,128)(2,1)S(1)} %copy.99.noi, s32[32,128]{1,0:T(8,128)} %bitcast.9, ...), custom_call_target="tpu_custom_call" | custom-call | tf_op jit(solution)/shard_map/pairing_plan/pallas_call | solution.py:595
  140.6 0.0 copy-start.1
  140.6 0.3 conditional.1
  140.9 0.0 copy-start.2
  140.9 1.3 broadcast_multiply_fusion
  142.2 0.0 copy-done.1
  142.2 0.8 copy.101
  143.0 0.0 copy-done.2
  (1 shorter events, 0.0 us)
Async XLA Ops:
  140.6 1.6 %copy-start.1 = (bf16[256,1024]{1,0:T(8,128)(2,1)S(1)}, bf16[256,1024]{1,0:T(8,128)(2,1)}, u32[]{:S(2)}) copy-start(bf16[256,1024]{1,0:T(8,128)(2,1)} %get-tuple-element.962) | copy-start | bytes 1572868
  140.9 2.1 %copy-start.2 = (f32[256]{0:T(256)}, f32[256]{0:T(256)S(1)}, u32[]{:S(2)}) copy-start(f32[256]{0:T(256)S(1)} %get-tuple-element.963) | copy-start | bytes 3076

commit v4 on v3

--- a/solution.py
+++ b/solution.py
@@ -30,7 +30,8 @@
         passing = next_one(passing, axis)
         return passing, join(total, passing)
 
-    return lax.fori_loop(1, lax.axis_size(axis), step, (value, value))[1]
+    passing = next_one(value, axis)
+    return lax.fori_loop(2, lax.axis_size(axis), step, (passing, join(value, passing)))[1]
 
 
 def whole(value, axis):
@@ -47,7 +48,9 @@
         return passing, put(out, passing, lax.rem(place + count - k, count))
 
     out = put(jnp.zeros((count * size,) + value.shape[1:], value.dtype), value, place)
-    return lax.fori_loop(1, count, step, (value, out))[1]
+    passing = next_one(value, axis)
+    out = put(out, passing, lax.rem(place + count - 1, count))
+    return lax.fori_loop(2, count, step, (passing, out))[1]
 
 
 def row_update(cost, potential, offset):
@@ -128,8 +131,8 @@
     lat, noi, req, bucket,
     out_f, out_g, out_w, out_c, out_bad, out_i,
     x_buf, y_buf, e_buf, s_buf, norm_y, wide, pick, send_rows, got_rows,
-    fx_got, fz_got, g_got, pg_got, peak, scale, rank, asked,
-    own_sem, x_send, x_recv, y_send, y_recv, fx_send, fx_recv, fz_send, fz_recv, g_send, g_recv,
+    f_got, g_got, pg_got, peak, scale, rank, asked,
+    own_sem, x_send, x_recv, y_send, y_recv, f_send, f_recv, g_send, g_recv,
     p_send, p_recv, q_send, q_recv,
 ):
     rows = 256
@@ -248,18 +251,11 @@
         for move in moves:
             y_copy(move, True).wait_recv()
 
-    def fx_copy(it, k):
+    def f_copy(it, k):
         return pltpu.make_async_remote_copy(
-            src_ref=fx_got.at[it, x], dst_ref=fx_got.at[it, x],
-            send_sem=fx_send.at[it, k], recv_sem=fx_recv.at[it, k],
-            device_id={"col": col_at(0, k)}, device_id_type=MESH,
-        )
-
-    def fz_copy(it, k):
-        return pltpu.make_async_remote_copy(
-            src_ref=fz_got.at[it, z], dst_ref=fz_got.at[it, z],
-            send_sem=fz_send.at[it, k], recv_sem=fz_recv.at[it, k],
-            device_id={"col": col_at(k, 0)}, device_id_type=MESH,
+            src_ref=f_got.at[it, col], dst_ref=f_got.at[it, col],
+            send_sem=f_send.at[it, k], recv_sem=f_recv.at[it, k],
+            device_id=col_peer(k), device_id_type=MESH,
         )
 
     def g_copy(it, k):
@@ -317,6 +313,13 @@
 
     own_x.wait()
     own_y.wait()
+
+    def norms(dy):
+        at = pl.multiple_of(row_at(dy, False) // 2 * (2 * rows), 2 * rows)
+        v = y_buf[pl.ds(row_at(dy, False) // 2 * 2, 2)].reshape(2 * rows, features).astype(F32)
+        n = jnp.sum(v * v, axis=1, keepdims=True) * unit
+        norm_y[pl.ds(at, 2 * rows), :] = jnp.broadcast_to(n, (2 * rows, 128))
+
     y_wait("+0")
     y_start("+f")
     y_wait("-1")
@@ -333,65 +336,84 @@
     y_start("sm")
     y_wait("-0")
     y_start("sp")
+    y_wait("s")
+    norms(0)
     for way in ("x+", "x-"):
         x_wait((way, "B"))
         x_start((way, "fB", 0))
     for way in ("z+", "z-"):
         x_wait((way, "A"))
         x_start((way, "fA", 0))
-    x_wait(("x+", "fA"), ("x-", "fA"))
-    x_start(("z+", "A", 2), ("z-", "A", 2))
-    x_wait(("z+", "fB"), ("z-", "fB"))
-    x_start(("x+", "B", 2), ("x-", "B", 2))
-    y_wait("+f")
-    y_start("s0")
-    y_wait("-f")
-    y_start("s1")
-    y_wait("s", "sm", "sp", "s0", "s1")
-
-    def norms(r, _):
-        v = y_buf[r].astype(F32)
-        n = jnp.sum(v * v, axis=1, keepdims=True) * unit
-        norm_y[pl.ds(pl.multiple_of(r * rows, rows), rows), :] = jnp.broadcast_to(n, (rows, 128))
-        return 0
-
-    lax.fori_loop(0, n_row, norms, 0)
-
-    def block(c):
-        latent = x_buf[c]
-        norm = norm_y[...]
-        t = dot_nt(y_buf[...].reshape(span, features), latent) * (2.0 * unit)
+    y_wait("sm", "sp")
+    norms(-1)
+    norms(1)
+
+    def score(c, at, count):
+        norm = norm_y[pl.ds(at, count), :]
+        draws = y_buf[pl.ds(at // rows, count // rows)].reshape(count, features)
+        t = dot_nt(draws, x_buf[c]) * (2.0 * unit)
         t = t - jnp.concatenate([norm, norm], axis=1)
-        s_buf[...] = t
-        top = jnp.max(jnp.max(t.reshape(span // 8, 8, rows), axis=0), axis=0, keepdims=True)
+        e_buf[c, pl.ds(at, count), :] = t
+        return jnp.max(t.reshape(count // 8, 8, rows), axis=0)
+
+    def powers(c, top):
+        top = jnp.max(top, axis=0, keepdims=True)
         peak[pl.ds(c, 1), :] = top
 
-        def powers(r, total):
+        def part(r, total):
             at = pl.multiple_of(r * 512, 512)
-            v = jnp.exp2(s_buf[pl.ds(at, 512), :] - top)
+            v = jnp.exp2(e_buf[c, pl.ds(at, 512), :] - top)
             e_buf[c, pl.ds(at, 512), :] = v
             return total + jnp.sum(v.reshape(64, 8, rows), axis=0)
 
-        total = lax.fori_loop(0, span // 512, powers, jnp.zeros((8, rows), F32))
-        fx_got[0, x, pl.ds(c, 1), :] = top + jnp.log2(jnp.sum(total, axis=0, keepdims=True))
+        total = lax.fori_loop(0, span // 512, part, jnp.zeros((8, rows), F32))
+        f_got[0, col, pl.ds(c, 1), :] = top + jnp.log2(jnp.sum(total, axis=0, keepdims=True))
+
+    def pair_at(dy):
+        return pl.multiple_of(row_at(dy, False) // 2 * (2 * rows), 2 * rows)
+
+    def early(c, k):
+        def part(d, top):
+            at = pl.multiple_of(lax.rem(y + 3 + d, 4) * (2 * rows), 2 * rows)
+            return jnp.maximum(top, score(c, at, 2 * rows))
+
+        s_buf[k] = lax.fori_loop(0, 3, part, jnp.full((8, rows), -3.0e38, F32))
+
+    def late(c, k):
+        powers(c, jnp.maximum(s_buf[k], score(c, pair_at(2), 2 * rows)))
+
+    def block(c, k):
+        powers(c, score(c, 0, span))
 
     near = (-1, 1)
     blocks = ((0, 0), (0, -1), (0, 1), (-1, 0), (1, 0), (-1, -1), (-1, 1), (1, -1), (1, 1),
-              (0, 2), (2, 0), (-1, 2), (1, 2), (2, -1), (2, 1), (2, 2))
-
-    def some_blocks(first, last):
+              (0, 2), (2, 0), (-1, 2), (2, -1), (1, 2), (2, 1), (2, 2))
+
+    def some_blocks(act, first, last):
         def step(k, _):
             dz = jnp.int32(0)
             dx = jnp.int32(0)
             for i in range(first, last):
                 dz = jnp.where(k == i, blocks[i][0], dz)
                 dx = jnp.where(k == i, blocks[i][1], dx)
-            block(lax.rem(z + dz + 8, 4) * 4 + lax.rem(x + dx + 8, 4))
+            act(lax.rem(z + dz + 8, 4) * 4 + lax.rem(x + dx + 8, 4), k)
             return 0
 
         lax.fori_loop(first, last, step, 0)
 
-    some_blocks(0, 4)
+    some_blocks(early, 0, 2)
+    y_wait("+f")
+    y_start("s0")
+    y_wait("-f")
+    y_start("s1")
+    some_blocks(early, 2, 5)
+    y_wait("s0", "s1")
+    norms(2)
+    some_blocks(late, 0, 5)
+    x_wait(("x+", "fA"), ("x-", "fA"))
+    x_start(("z+", "A", 2), ("z-", "A", 2))
+    x_wait(("z+", "fB"), ("z-", "fB"))
+    x_start(("x+", "B", 2), ("x-", "B", 2))
     for d in near:
         for way in ("x+", "x-"):
             x_wait((way, "B", d))
@@ -399,21 +421,21 @@
         for way in ("z+", "z-"):
             x_wait((way, "A", d))
             x_start((way, "fA", d))
-    some_blocks(4, 8)
+    some_blocks(block, 5, 9)
+    x_wait(("x+", "fB", 0), ("x-", "fB", 0), ("z+", "fA", 0), ("z-", "fA", 0))
+    some_blocks(block, 9, 11)
     for way in ("x+", "x-"):
         x_wait((way, "B", 2))
         x_start((way, "fB", 2))
     for way in ("z+", "z-"):
         x_wait((way, "A", 2))
         x_start((way, "fA", 2))
-    some_blocks(8, 9)
-    x_wait(("x+", "fB", 0), ("x-", "fB", 0), ("z+", "fA", 0), ("z-", "fA", 0))
-    some_blocks(9, 11)
-    for d in near:
-        x_wait(("x+", "fB", d), ("x-", "fB", d), ("z+", "fA", d), ("z-", "fA", d))
-    some_blocks(11, 15)
+    x_wait(("x+", "fB", -1), ("x-", "fB", -1), ("z+", "fA", -1), ("z-", "fA", -1))
+    some_blocks(block, 11, 13)
+    x_wait(("x+", "fB", 1), ("x-", "fB", 1), ("z+", "fA", 1), ("z-", "fA", 1))
+    some_blocks(block, 13, 15)
     x_wait(("x+", "fB", 2), ("x-", "fB", 2), ("z+", "fA", 2), ("z-", "fA", 2))
-    some_blocks(15, 16)
+    some_blocks(block, 15, 16)
 
     def in_range(v):
         return (v >= LOW) & (v <= HIGH)
@@ -443,12 +465,14 @@
 
         acc = lax.fori_loop(0, span // 128, body, tuple(jnp.zeros((8, rows), F32) for _ in range(n_col)))
         for c in range(n_col):
-            fx_got[it, x, c : c + 1, :] = jnp.sum(acc[c], axis=0, keepdims=True) * scale[n_col + c : n_col + c + 1, :]
+            f_got[it, col, c : c + 1, :] = jnp.sum(acc[c], axis=0, keepdims=True) * scale[n_col + c : n_col + c + 1, :]
 
     def log_sum(ref, it):
-        top = jnp.maximum(jnp.maximum(ref[it, 0], ref[it, 1]), jnp.maximum(ref[it, 2], ref[it, 3]))
+        top = ref[it, 0]
+        for d in range(1, n_col):
+            top = jnp.maximum(top, ref[it, d])
         total = jnp.exp2(ref[it, 0] - top)
-        for d in range(1, 4):
+        for d in range(1, n_col):
             total = total + jnp.exp2(ref[it, d] - top)
         return top + jnp.log2(total)
 
@@ -470,25 +494,57 @@
         lax.fori_loop(0, n_col // 4, fill, 0)
         got_rows[col] = send_rows[col]
 
+    def unpack():
+        each(n_col, lambda k: p_copy(k).wait_recv())
+        mine = asked[pl.ds(col, 1), :]
+        anchor = mine // span
+        marker = lax.broadcasted_iota(jnp.int32, (n_col, rows), 0) == anchor
+        marked = marker.astype(F32)
+        spot = jnp.sum(marked * dot_nn(marked.astype(BF16), before), axis=0, keepdims=True)
+        flat = anchor.astype(F32) * 32.0 + spot
+        tick = (bucket[...].astype(F32) + 0.5) / BUCKETS
+        lanes = lax.broadcasted_iota(jnp.int32, (128, 32 * n_col), 1).astype(F32)
+        costs = []
+        squares = []
+        for h in range(2):
+            flat_h = spread_rows(flat[:, h * 128 : (h + 1) * 128])
+            take = (lanes == flat_h[:, :1]).astype(F32).astype(BF16)
+            paired = dot_nn(take, got_rows[...].reshape(32 * n_col, features))
+            data = x_buf[col, h * 128 : (h + 1) * 128, :].astype(F32)
+            t = spread_rows(tick[:, h * 128 : (h + 1) * 128])[:, :1]
+            out_i[h * 128 : (h + 1) * 128, :] = ((1.0 - t) * data + t * paired).astype(BF16)
+            diff = data - paired
+            cost = diff * diff
+            square = data * data
+            fold_c = cost[:, :128]
+            fold_s = square[:, :128]
+            for q in range(1, features // 128):
+                fold_c = fold_c + cost[:, q * 128 : (q + 1) * 128]
+                fold_s = fold_s + square[:, q * 128 : (q + 1) * 128]
+            costs.append(turn_to_lanes(fold_c))
+            squares.append(turn_to_lanes(fold_s))
+        pair_cost = jnp.concatenate(costs, axis=1) / features
+        norm_x = jnp.concatenate(squares, axis=1) / features
+        return spot, marker, pair_cost, norm_x
+
     big_q = None
     for it in range(ITERS):
         if it > 0:
             row_pass(it)
-        each(4, lambda k: fx_copy(it, k).start())
+        each(n_col, lambda k: f_copy(it, k).start())
         if it == 0:
             prepare()
-        each(4, lambda k: fx_copy(it, k).wait_recv())
-        fz_got[it, z] = log_sum(fx_got, it) if it == 0 else summed(fx_got, it, 4)
-        each(4, lambda k: fz_copy(it, k).start())
-        each(4, lambda k: fz_copy(it, k).wait_recv())
+        if it == ITERS - 1:
+            spot, marker, pair_cost, norm_x = unpack()
+        each(n_col, lambda k: f_copy(it, k).wait_recv())
         if it == 0:
-            lse = log_sum(fz_got, it)
+            lse = log_sum(f_got, it)
             rank[0:n_col, :] = lse
             weight = jnp.exp2(peak[...] - lse)
             scale[n_col : 2 * n_col, :] = weight
             scale[0:n_col, :] = weight
         else:
-            total = summed(fz_got, it, 4)
+            total = summed(f_got, it, n_col)
             a = jnp.where(in_range(total), 1.0 / total, jnp.nan)
             scale[0:n_col, :] = a * scale[n_col : 2 * n_col, :]
             if it == ITERS - 1:
@@ -498,37 +554,6 @@
         if it < ITERS - 1:
             for k in range(1 + 5 * it, 6 + 5 * it):
                 p_copy(k).start()
-        if it == ITERS - 1:
-            each(n_col, lambda k: p_copy(k).wait_recv())
-            mine = asked[pl.ds(col, 1), :]
-            anchor = mine // span
-            marker = lax.broadcasted_iota(jnp.int32, (n_col, rows), 0) == anchor
-            marked = marker.astype(F32)
-            spot = jnp.sum(marked * dot_nn(marked.astype(BF16), before), axis=0, keepdims=True)
-            flat = anchor.astype(F32) * 32.0 + spot
-            tick = (bucket[...].astype(F32) + 0.5) / BUCKETS
-            lanes = lax.broadcasted_iota(jnp.int32, (128, 32 * n_col), 1).astype(F32)
-            costs = []
-            squares = []
-            for h in range(2):
-                flat_h = spread_rows(flat[:, h * 128 : (h + 1) * 128])
-                take = (lanes == flat_h[:, :1]).astype(F32).astype(BF16)
-                paired = dot_nn(take, got_rows[...].reshape(32 * n_col, features))
-                data = x_buf[col, h * 128 : (h + 1) * 128, :].astype(F32)
-                t = spread_rows(tick[:, h * 128 : (h + 1) * 128])[:, :1]
-                out_i[h * 128 : (h + 1) * 128, :] = ((1.0 - t) * data + t * paired).astype(BF16)
-                diff = data - paired
-                cost = diff * diff
-                square = data * data
-                fold_c = cost[:, :128]
-                fold_s = square[:, :128]
-                for q in range(1, features // 128):
-                    fold_c = fold_c + cost[:, q * 128 : (q + 1) * 128]
-                    fold_s = fold_s + square[:, q * 128 : (q + 1) * 128]
-                costs.append(turn_to_lanes(fold_c))
-                squares.append(turn_to_lanes(fold_s))
-            pair_cost = jnp.concatenate(costs, axis=1) / features
-            norm_x = jnp.concatenate(squares, axis=1) / features
         each(n_row, lambda k: g_copy(it, k).wait_recv())
         big_q = summed(g_got, it, n_row)
         if it < ITERS - 1:
@@ -540,13 +565,16 @@
 
     fine = jnp.min(jnp.where(in_range(big_q), 1.0, 0.0), axis=(0, 1), keepdims=True)
     g = jnp.where(fine > 0.0, jnp.log(big_q), jnp.nan)
-    chosen = [jnp.zeros((8, 32 * n_col), F32)]
-    for part in three_parts(g):
-        for r in range(n_row):
-            one = jnp.broadcast_to(part[r : r + 1, :], (8, rows))
-            chosen[0] = chosen[0] + dot_nt(one, pick[:, r * rows : (r + 1) * rows])
+    parts = three_parts(g)
+    chosen = jnp.zeros((8, 32 * n_col), F32)
+    for r in range(n_row):
+        three = jnp.concatenate(
+            [p[r : r + 1, :].astype(F32) for p in parts] + [jnp.zeros((5, rows), F32)], axis=0
+        ).astype(BF16)
+        chosen = chosen + dot_nt(three, pick[:, r * rows : (r + 1) * rows])
+    chosen = jnp.sum(chosen, axis=0, keepdims=True)
     for q in range(n_col // 4):
-        pg_got[n_col + q] = chosen[0][:1, q * 128 : (q + 1) * 128]
+        pg_got[n_col + q] = chosen[:, q * 128 : (q + 1) * 128]
     each(n_col, lambda k: q_copy(k).start())
     pg_got[col] = pg_got[n_col + col // 4]
     log_total = math.log(total_rows)
@@ -577,8 +605,7 @@
     each(n_col, lambda k: p_copy(k).wait_send())
     each(n_col, lambda k: q_copy(k).wait_send())
     for it in range(ITERS):
-        each(4, lambda k: fx_copy(it, k).wait_send())
-        each(4, lambda k: fz_copy(it, k).wait_send())
+        each(n_col, lambda k: f_copy(it, k).wait_send())
         each(n_row, lambda k: g_copy(it, k).wait_send())
 
 
@@ -605,14 +632,13 @@
             pltpu.VMEM((n_col, own_rows, features), BF16),
             pltpu.VMEM((n_row, own_rows, features), BF16),
             pltpu.VMEM((n_col, span, own_rows), F32),
-            pltpu.VMEM((span, own_rows), F32),
+            pltpu.VMEM((8, 8, own_rows), F32),
             pltpu.VMEM((span, 128), F32),
             pltpu.VMEM((span, 128), F32),
             pltpu.VMEM((32 * n_col, span), BF16),
             pltpu.VMEM((n_col, 32, features), BF16),
             pltpu.VMEM((n_col, 32, features), BF16),
-            pltpu.VMEM((ITERS, 4, n_col, own_rows), F32),
-            pltpu.VMEM((ITERS, 4, n_col, own_rows), F32),
+            pltpu.VMEM((ITERS, n_col, n_col, own_rows), F32),
             pltpu.VMEM((ITERS, n_row, n_row, own_rows), F32),
             pltpu.VMEM((n_col + n_col // 4, 1, 128), F32),
             pltpu.VMEM((n_col, own_rows), F32),
@@ -622,8 +648,7 @@
             dma((2,)),
             dma((40,)), dma((40,)),
             dma((11,)), dma((11,)),
-            dma((ITERS, 4)), dma((ITERS, 4)),
-            dma((ITERS, 4)), dma((ITERS, 4)),
+            dma((ITERS, n_col)), dma((ITERS, n_col)),
             dma((ITERS, n_row)), dma((ITERS, n_row)),
             dma((n_col,)), dma((n_col,)),
             dma((n_col,)), dma((n_col,)),

time: 143 us -> 128 us (0.90)
  Pallas kernels: 137 us -> 124 us
  local copies, waits for them, and re-layouts: 2.89 us -> 0.8 us
    pallas_call x1, Pallas kernels: 137 us -> 124 us  [shards(): pl.pallas_call(functools.partial(kernel, n_row, n_col, features, total_ro...]
    unnamed x7 -> x5, local copies, waits for them, and re-layouts: 2.89 us -> 0.8 us
where the time goes in v4:
time: 128 us
  Pallas kernels  124 us (97%)
  between operations  1.35 us (1%)
    pallas_call x1, Pallas kernels, shards(): pl.pallas_call(functools.partial(kernel, n_row, n_col, features, total_ro...  124 us

profile of v4, /device:TPU:1, one launch (start us, length us, event | category | flops | bytes accessed | tf_op | source)
XLA Modules:
  0.0 128.0 jit_solution(2639157362876007029)
XLA Ops:
  0.6 124.3 %pairing_plan.1 = (f32[1,256]{1,0:T(1,128)}, f32[1,256]{1,0:T(1,128)}, f32[1,256]{1,0:T(1,128)S(1)}, f32[1,256]{1,0:T(1,128)}, s32[1,1]{1,0:T(1,128)}, /*index=5*/bf16[256,1024]{1,0:T(8,128)(2,1)}) custom-call(bf16[256,1024]{1,0:T(8,128)(2,1)} %lat.1, bf16[256,1024]{1,0:T(8,128)(2,1)} %noi.1, s32[32,128]{1,0:T(8,128)} %bitcast.9, s32[1,256]{1,0:T(1,128)} %bitcast.10), custom_call_target="tpu_custom_call" | custom-call | tf_op jit(solution)/shard_map/pairing_plan/pallas_call | solution.py:622
  125.6 0.0 copy-start.3
  125.6 0.3 conditional.1
  125.9 0.0 copy-start.4
  125.9 1.3 broadcast_multiply_fusion
  127.2 0.0 copy-done.3
  127.2 0.8 copy.100
  128.0 0.0 copy-done.4
  (1 shorter events, 0.0 us)
Async XLA Ops:
  125.6 1.6 %copy-start.3 = (bf16[256,1024]{1,0:T(8,128)(2,1)S(1)}, bf16[256,1024]{1,0:T(8,128)(2,1)}, u32[]{:S(2)}) copy-start(bf16[256,1024]{1,0:T(8,128)(2,1)} %get-tuple-element.971) | copy-start | bytes 1572868
  125.9 2.1 %copy-start.4 = (f32[256]{0:T(256)}, f32[256]{0:T(256)S(1)}, u32[]{:S(2)}) copy-start(f32[256]{0:T(256)S(1)} %get-tuple-element.972) | copy-start | bytes 3076

commit v5 on v4

--- a/solution.py
+++ b/solution.py
@@ -137,6 +137,8 @@
 ):
     rows = 256
     span = n_row * rows
+    f_half = n_col // 2
+    g_half = n_row // 2
     row = lax.axis_index("row")
     col = lax.axis_index("col")
     log2e = math.log2(math.e)
@@ -251,17 +253,19 @@
         for move in moves:
             y_copy(move, True).wait_recv()
 
-    def f_copy(it, k):
+    def f_copy(it, k, h):
+        place = f_got.at[it, col, pl.ds(h * f_half, f_half)]
         return pltpu.make_async_remote_copy(
-            src_ref=f_got.at[it, col], dst_ref=f_got.at[it, col],
-            send_sem=f_send.at[it, k], recv_sem=f_recv.at[it, k],
+            src_ref=place, dst_ref=place,
+            send_sem=f_send.at[it, 2 * k + h], recv_sem=f_recv.at[it, 2 * k + h],
             device_id=col_peer(k), device_id_type=MESH,
         )
 
-    def g_copy(it, k):
+    def g_copy(it, k, h):
+        place = g_got.at[it, h, row]
         return pltpu.make_async_remote_copy(
-            src_ref=g_got.at[it, row], dst_ref=g_got.at[it, row],
-            send_sem=g_send.at[it, k], recv_sem=g_recv.at[it, k],
+            src_ref=place, dst_ref=place,
+            send_sem=g_send.at[it, 2 * k + h], recv_sem=g_recv.at[it, 2 * k + h],
             device_id=row_peer(k), device_id_type=MESH,
         )
 
@@ -440,47 +444,89 @@
     def in_range(v):
         return (v >= LOW) & (v <= HIGH)
 
-    def column_pass(it):
+    def column_sums(first, last, start, count):
         def body(q, _):
-            at = pl.multiple_of(q * 256, 256)
+            at = pl.multiple_of(start + q * 256, 256)
             total = jnp.zeros((256, rows), F32)
-            for c in range(n_col):
+            for c in range(first, last):
                 total = total + e_buf[c, pl.ds(at, 256), :] * scale[c : c + 1, :]
-            wide[pl.ds(at, 256), :] = total[:, :128] + total[:, 128:]
+            total = total[:, :128] + total[:, 128:]
+            if first > 0:
+                total = total + wide[pl.ds(at, 256), :]
+            wide[pl.ds(at, 256), :] = total
             return 0
 
-        lax.fori_loop(0, span // 256, body, 0)
-        for r in range(n_row):
-            g_got[it, row, r : r + 1, :] = turn_to_lanes(wide[r * rows : (r + 1) * rows, :])
-
-    def row_pass(it):
+        lax.fori_loop(0, count // 256, body, 0)
+
+    def row_sums(first, last, start, count, acc):
         def body(j, acc):
-            at = pl.multiple_of(j * 128, 128)
+            at = pl.multiple_of(start + j * 128, 128)
             b = wide[pl.ds(at, 128), :]
             b = jnp.concatenate([b, b], axis=1)
             return tuple(
-                acc[c] + jnp.sum((e_buf[c, pl.ds(at, 128), :] * b).reshape(16, 8, rows), axis=0)
-                for c in range(n_col)
+                acc[c - first] + jnp.sum((e_buf[c, pl.ds(at, 128), :] * b).reshape(16, 8, rows), axis=0)
+                for c in range(first, last)
             )
 
-        acc = lax.fori_loop(0, span // 128, body, tuple(jnp.zeros((8, rows), F32) for _ in range(n_col)))
-        for c in range(n_col):
-            f_got[it, col, c : c + 1, :] = jnp.sum(acc[c], axis=0, keepdims=True) * scale[n_col + c : n_col + c + 1, :]
-
-    def log_sum(ref, it):
-        top = ref[it, 0]
-        for d in range(1, n_col):
-            top = jnp.maximum(top, ref[it, d])
-        total = jnp.exp2(ref[it, 0] - top)
-        for d in range(1, n_col):
-            total = total + jnp.exp2(ref[it, d] - top)
+        return lax.fori_loop(0, count // 128, body, acc)
+
+    def log_sum(parts):
+        top = parts[0]
+        for part in parts[1:]:
+            top = jnp.maximum(top, part)
+        total = jnp.exp2(parts[0] - top)
+        for part in parts[1:]:
+            total = total + jnp.exp2(part - top)
         return top + jnp.log2(total)
 
-    def summed(ref, it, n):
-        total = ref[it, 0]
-        for d in range(1, n):
-            total = total + ref[it, d]
+    def summed(parts):
+        total = parts[0]
+        for part in parts[1:]:
+            total = total + part
         return total
+
+    def f_arrived(it, h):
+        each(n_col, lambda k: f_copy(it, k, h).wait_recv())
+        lo, hi = h * f_half, (h + 1) * f_half
+        parts = [f_got[it, d, lo:hi] for d in range(n_col)]
+        if it == 0:
+            lse = log_sum(parts)
+            rank[lo:hi, :] = lse
+            weight = jnp.exp2(peak[lo:hi, :] - lse)
+            scale[n_col + lo : n_col + hi, :] = weight
+            scale[lo:hi, :] = weight
+        else:
+            total = summed(parts)
+            a = jnp.where(in_range(total), 1.0 / total, jnp.nan)
+            scale[lo:hi, :] = a * scale[n_col + lo : n_col + hi, :]
+            if it == ITERS - 1:
+                rank[n_col + lo : n_col + hi, :] = total
+
+    def g_arrived(it, h):
+        each(n_row, lambda k: g_copy(it, k, h).wait_recv())
+        return summed([g_got[it, h, d] for d in range(n_row)])
+
+    def g_spread(it, h):
+        total = g_arrived(it, h)
+        b = jnp.where(in_range(total), 1.0 / total, jnp.nan)
+        for r in range(g_half):
+            for q in range(2):
+                at = (h * g_half + r) * rows + q * 128
+                wide[at : at + 128, :] = spread_rows(b[r : r + 1, q * 128 : (q + 1) * 128])
+
+    def f_leave(it, h, acc):
+        for i in range(f_half):
+            c = h * f_half + i
+            f_got[it, col, c : c + 1, :] = (
+                jnp.sum(acc[i], axis=0, keepdims=True) * scale[n_col + c : n_col + c + 1, :]
+            )
+        each(n_col, lambda k: f_copy(it, k, h).start())
+
+    def g_leave(it, h):
+        for i in range(g_half):
+            at = (h * g_half + i) * rows
+            g_got[it, h, row, i : i + 1, :] = turn_to_lanes(wide[at : at + rows, :])
+        each(n_row, lambda k: g_copy(it, k, h).start())
 
     def prepare():
         def fill(q, _):
@@ -494,74 +540,64 @@
         lax.fori_loop(0, n_col // 4, fill, 0)
         got_rows[col] = send_rows[col]
 
-    def unpack():
-        each(n_col, lambda k: p_copy(k).wait_recv())
+    def own_slots():
         mine = asked[pl.ds(col, 1), :]
         anchor = mine // span
         marker = lax.broadcasted_iota(jnp.int32, (n_col, rows), 0) == anchor
         marked = marker.astype(F32)
         spot = jnp.sum(marked * dot_nn(marked.astype(BF16), before), axis=0, keepdims=True)
-        flat = anchor.astype(F32) * 32.0 + spot
-        tick = (bucket[...].astype(F32) + 0.5) / BUCKETS
+        return marker, spot, anchor.astype(F32) * 32.0 + spot
+
+    def unpack(h, flat):
+        tick = (bucket[:, h * 128 : (h + 1) * 128].astype(F32) + 0.5) / BUCKETS
         lanes = lax.broadcasted_iota(jnp.int32, (128, 32 * n_col), 1).astype(F32)
-        costs = []
-        squares = []
-        for h in range(2):
-            flat_h = spread_rows(flat[:, h * 128 : (h + 1) * 128])
-            take = (lanes == flat_h[:, :1]).astype(F32).astype(BF16)
-            paired = dot_nn(take, got_rows[...].reshape(32 * n_col, features))
-            data = x_buf[col, h * 128 : (h + 1) * 128, :].astype(F32)
-            t = spread_rows(tick[:, h * 128 : (h + 1) * 128])[:, :1]
-            out_i[h * 128 : (h + 1) * 128, :] = ((1.0 - t) * data + t * paired).astype(BF16)
-            diff = data - paired
-            cost = diff * diff
-            square = data * data
-            fold_c = cost[:, :128]
-            fold_s = square[:, :128]
-            for q in range(1, features // 128):
-                fold_c = fold_c + cost[:, q * 128 : (q + 1) * 128]
-                fold_s = fold_s + square[:, q * 128 : (q + 1) * 128]
-            costs.append(turn_to_lanes(fold_c))
-            squares.append(turn_to_lanes(fold_s))
-        pair_cost = jnp.concatenate(costs, axis=1) / features
-        norm_x = jnp.concatenate(squares, axis=1) / features
-        return spot, marker, pair_cost, norm_x
-
-    big_q = None
+        flat_h = spread_rows(flat[:, h * 128 : (h + 1) * 128])
+        take = (lanes == flat_h[:, :1]).astype(F32).astype(BF16)
+        paired = dot_nn(take, got_rows[...].reshape(32 * n_col, features))
+        data = x_buf[col, h * 128 : (h + 1) * 128, :].astype(F32)
+        t = spread_rows(tick)[:, :1]
+        out_i[h * 128 : (h + 1) * 128, :] = ((1.0 - t) * data + t * paired).astype(BF16)
+        diff = data - paired
+        cost = diff * diff
+        square = data * data
+        fold_c = cost[:, :128]
+        fold_s = square[:, :128]
+        for q in range(1, features // 128):
+            fold_c = fold_c + cost[:, q * 128 : (q + 1) * 128]
+            fold_s = fold_s + square[:, q * 128 : (q + 1) * 128]
+        return turn_to_lanes(fold_c) / features, turn_to_lanes(fold_s) / features
+
+    half_span = span // 2
+    empty = tuple(jnp.zeros((8, rows), F32) for _ in range(n_col))
     for it in range(ITERS):
-        if it > 0:
-            row_pass(it)
-        each(n_col, lambda k: f_copy(it, k).start())
         if it == 0:
+            for h in range(2):
+                each(n_col, lambda k: f_copy(it, k, h).start())
             prepare()
+        else:
+            g_spread(it - 1, 0)
+            acc = row_sums(0, n_col, 0, half_span, empty)
+            g_spread(it - 1, 1)
+            f_leave(it, 0, row_sums(0, f_half, half_span, half_span, acc[:f_half]))
+            f_leave(it, 1, row_sums(f_half, n_col, half_span, half_span, acc[f_half:]))
         if it == ITERS - 1:
-            spot, marker, pair_cost, norm_x = unpack()
-        each(n_col, lambda k: f_copy(it, k).wait_recv())
-        if it == 0:
-            lse = log_sum(f_got, it)
-            rank[0:n_col, :] = lse
-            weight = jnp.exp2(peak[...] - lse)
-            scale[n_col : 2 * n_col, :] = weight
-            scale[0:n_col, :] = weight
-        else:
-            total = summed(f_got, it, n_col)
-            a = jnp.where(in_range(total), 1.0 / total, jnp.nan)
-            scale[0:n_col, :] = a * scale[n_col : 2 * n_col, :]
-            if it == ITERS - 1:
-                rank[n_col : 2 * n_col, :] = total
-        column_pass(it)
-        each(n_row, lambda k: g_copy(it, k).start())
+            each(n_col, lambda k: p_copy(k).wait_recv())
+            marker, spot, flat = own_slots()
+            cost_a, square_a = unpack(0, flat)
+        f_arrived(it, 0)
+        column_sums(0, f_half, 0, span)
+        f_arrived(it, 1)
+        column_sums(f_half, n_col, 0, half_span)
+        g_leave(it, 0)
+        column_sums(f_half, n_col, half_span, half_span)
+        g_leave(it, 1)
         if it < ITERS - 1:
             for k in range(1 + 5 * it, 6 + 5 * it):
                 p_copy(k).start()
-        each(n_row, lambda k: g_copy(it, k).wait_recv())
-        big_q = summed(g_got, it, n_row)
-        if it < ITERS - 1:
-            b = jnp.where(in_range(big_q), 1.0 / big_q, jnp.nan)
-            for r in range(n_row):
-                for h in range(2):
-                    at = r * rows + h * 128
-                    wide[at : at + 128, :] = spread_rows(b[r : r + 1, h * 128 : (h + 1) * 128])
+    cost_b, square_b = unpack(1, flat)
+    pair_cost = jnp.concatenate([cost_a, cost_b], axis=1)
+    norm_x = jnp.concatenate([square_a, square_b], axis=1)
+    big_q = jnp.concatenate([g_arrived(ITERS - 1, 0), g_arrived(ITERS - 1, 1)], axis=0)
 
     fine = jnp.min(jnp.where(in_range(big_q), 1.0, 0.0), axis=(0, 1), keepdims=True)
     g = jnp.where(fine > 0.0, jnp.log(big_q), jnp.nan)
@@ -605,8 +641,9 @@
     each(n_col, lambda k: p_copy(k).wait_send())
     each(n_col, lambda k: q_copy(k).wait_send())
     for it in range(ITERS):
-        each(n_col, lambda k: f_copy(it, k).wait_send())
-        each(n_row, lambda k: g_copy(it, k).wait_send())
+        for h in range(2):
+            each(n_col, lambda k: f_copy(it, k, h).wait_send())
+            each(n_row, lambda k: g_copy(it, k, h).wait_send())
 
 
 def shards(latents, noise, pairing, time_bucket):
@@ -639,7 +676,7 @@
             pltpu.VMEM((n_col, 32, features), BF16),
             pltpu.VMEM((n_col, 32, features), BF16),
             pltpu.VMEM((ITERS, n_col, n_col, own_rows), F32),
-            pltpu.VMEM((ITERS, n_row, n_row, own_rows), F32),
+            pltpu.VMEM((ITERS, 2, n_row, n_row // 2, own_rows), F32),
             pltpu.VMEM((n_col + n_col // 4, 1, 128), F32),
             pltpu.VMEM((n_col, own_rows), F32),
             pltpu.VMEM((2 * n_col, own_rows), F32),
@@ -648,8 +685,8 @@
             dma((2,)),
             dma((40,)), dma((40,)),
             dma((11,)), dma((11,)),
-            dma((ITERS, n_col)), dma((ITERS, n_col)),
-            dma((ITERS, n_row)), dma((ITERS, n_row)),
+            dma((ITERS, 2 * n_col)), dma((ITERS, 2 * n_col)),
+            dma((ITERS, 2 * n_row)), dma((ITERS, 2 * n_row)),
             dma((n_col,)), dma((n_col,)),
             dma((n_col,)), dma((n_col,)),
         ],

time: 128 us -> 125 us (0.977)
  Pallas kernels: 124 us -> 121 us
    pallas_call x1, Pallas kernels: 124 us -> 121 us  [shards(): pl.pallas_call(functools.partial(kernel, n_row, n_col, features, total_ro...]
where the time goes in v5:
time: 125 us
  Pallas kernels  121 us (97%)
  between operations  1.35 us (1%)
  other arithmetic  1.26 us (1%)
    pallas_call x1, Pallas kernels, shards(): pl.pallas_call(functools.partial(kernel, n_row, n_col, features, total_ro...  121 us

profile of v5, /device:TPU:1, one launch (start us, length us, event | category | flops | bytes accessed | tf_op | source)
XLA Modules:
  0.0 124.9 jit_solution(3078468417732800927)
XLA Ops:
  0.6 121.2 %pairing_plan.1 = (f32[1,256]{1,0:T(1,128)}, f32[1,256]{1,0:T(1,128)}, f32[1,256]{1,0:T(1,128)S(1)}, f32[1,256]{1,0:T(1,128)}, s32[1,1]{1,0:T(1,128)}, /*index=5*/bf16[256,1024]{1,0:T(8,128)(2,1)}) custom-call(bf16[256,1024]{1,0:T(8,128)(2,1)} %lat.1, bf16[256,1024]{1,0:T(8,128)(2,1)} %noi.1, s32[32,128]{1,0:T(8,128)} %bitcast.9, s32[1,256]{1,0:T(1,128)} %bitcast.10), custom_call_target="tpu_custom_call" | custom-call | tf_op jit(solution)/shard_map/pairing_plan/pallas_call | solution.py:659
  122.6 0.0 copy-start.3
  122.6 0.3 conditional.1
  122.9 0.0 copy-start.4
  122.9 1.3 %broadcast_multiply_fusion = (f32[256]{0:T(256)}, f32[256]{0:T(256)}) fusion(f32[256]{0:T(256)} %get-tuple-element.498, f32[256]{0:T(256)} %get-tuple-element.497), kind=kLoop, calls=%fused_computation.24 | loop fusion | flops 512 | bytes 4096 | tf_op jit(solution)/shard_map/mul | solution.py:705
  124.1 0.0 copy-done.3
  124.1 0.8 copy.100
  124.9 0.0 copy-done.4
  (1 shorter events, 0.0 us)
Async XLA Ops:
  122.6 1.6 %copy-start.3 = (bf16[256,1024]{1,0:T(8,128)(2,1)S(1)}, bf16[256,1024]{1,0:T(8,128)(2,1)}, u32[]{:S(2)}) copy-start(bf16[256,1024]{1,0:T(8,128)(2,1)} %get-tuple-element.971) | copy-start | bytes 1572868
  122.9 2.1 %copy-start.4 = (f32[256]{0:T(256)}, f32[256]{0:T(256)S(1)}, u32[]{:S(2)}) copy-start(f32[256]{0:T(256)S(1)} %get-tuple-element.972) | copy-start | bytes 3076

commit v6 on v5

--- a/solution.py
+++ b/solution.py
@@ -128,10 +128,10 @@
 
 def kernel(
     n_row, n_col, features, total_rows,
-    lat, noi, req, bucket,
-    out_f, out_g, out_w, out_c, out_bad, out_i,
+    lat, noi, req_in, bucket_in,
+    out_f, out_g, out_w, out_c, out_bad, out_all,
     x_buf, y_buf, e_buf, s_buf, norm_y, wide, pick, send_rows, got_rows,
-    f_got, g_got, pg_got, peak, scale, rank, asked,
+    f_got, g_got, pg_got, peak, scale, rank, asked, req, bucket, out_i,
     own_sem, x_send, x_recv, y_send, y_recv, f_send, f_recv, g_send, g_recv,
     p_send, p_recv, q_send, q_recv,
 ):
@@ -144,35 +144,40 @@
     log2e = math.log2(math.e)
     unit = log2e / (features * entropic)
 
+    z, x = col // 4, lax.rem(col, 4)
+    y, core = row // 2, lax.rem(row, 2)
+
+    def col_at(dz, dx):
+        return lax.rem(z + (dz + 8), 4) * 4 + lax.rem(x + (dx + 8), 4)
+
+    def row_at(dy, other):
+        return lax.rem(y + (dy + 8), 4) * 2 + (1 - core if other else core)
+
+    col_order = sorted(range(1, n_col), key=lambda k: -(min(k // 4, 4 - k // 4) + min(k % 4, 4 - k % 4)))
+    row_order = sorted(range(1, n_row), key=lambda k: -(2 * min(k // 2, 4 - k // 2) + k % 2))
+
+    def col_of(k):
+        return col_at(k // 4, k % 4)
+
     def col_peer(k):
-        return {"col": lax.rem(col + k, n_col)}
+        return {"col": col_of(k)}
 
     def row_peer(k):
-        return {"row": lax.rem(row + k, n_row)}
+        return {"row": row_at(k // 2, k % 2 == 1)}
 
     barrier = pltpu.get_barrier_semaphore()
 
-    def greet_col(k, _):
-        pl.semaphore_signal(barrier, inc=1, device_id=col_peer(k), device_id_type=MESH)
-        return 0
-
-    def greet_row(k, _):
-        pl.semaphore_signal(barrier, inc=1, device_id=row_peer(k), device_id_type=MESH)
-        return 0
-
-    lax.fori_loop(1, n_col, greet_col, 0)
-    lax.fori_loop(1, n_row, greet_row, 0)
+    for peer in [col_peer(k) for k in col_order] + [row_peer(k) for k in row_order]:
+        pl.semaphore_signal(barrier, inc=1, device_id=peer, device_id_type=MESH)
     own_x = pltpu.make_async_copy(lat, x_buf.at[col], own_sem.at[0])
     own_y = pltpu.make_async_copy(noi, y_buf.at[row], own_sem.at[1])
+    own_req = pltpu.make_async_copy(req_in, req, own_sem.at[2])
+    own_bucket = pltpu.make_async_copy(bucket_in, bucket, own_sem.at[3])
     own_x.start()
     own_y.start()
+    own_req.start()
+    own_bucket.start()
     pl.semaphore_wait(barrier, n_col + n_row - 2)
-
-    z, x = col // 4, lax.rem(col, 4)
-    y, core = row // 2, lax.rem(row, 2)
-
-    def col_at(dz, dx):
-        return lax.rem(z + (dz + 8), 4) * 4 + lax.rem(x + (dx + 8), 4)
 
     steps = {"x+": (0, 1), "x-": (0, -1), "z+": (1, 0), "z-": (-1, 0)}
     half = rows // 2
@@ -221,9 +226,6 @@
         for move in moves:
             x_copy(move, True).wait_recv()
 
-    def row_at(dy, other):
-        return lax.rem(y + (dy + 8), 4) * 2 + (1 - core if other else core)
-
     y_moves = {
         "+0": (1, 0, 0, half), "-1": (-1, 0, half, half),
         "+1": (1, 0, half, half), "-0": (-1, 0, 0, half),
@@ -271,20 +273,20 @@
 
     def p_copy(k):
         return pltpu.make_async_remote_copy(
-            src_ref=send_rows.at[lax.rem(col + k, n_col)], dst_ref=got_rows.at[col],
+            src_ref=send_rows.at[col_of(k)], dst_ref=got_rows.at[col],
             send_sem=p_send.at[k], recv_sem=p_recv.at[k],
             device_id=col_peer(k), device_id_type=MESH,
         )
 
     def q_copy(k):
         return pltpu.make_async_remote_copy(
-            src_ref=pg_got.at[n_col + lax.rem(col + k, n_col) // 4], dst_ref=pg_got.at[col],
+            src_ref=pg_got.at[n_col + col_of(k) // 4], dst_ref=pg_got.at[col],
             send_sem=q_send.at[k], recv_sem=q_recv.at[k],
             device_id=col_peer(k), device_id_type=MESH,
         )
 
     def each(n, act):
-        for k in range(1, n):
+        for k in col_order if n == n_col else row_order:
             act(k)
 
     y_start("+0", "-1", "s")
@@ -292,6 +294,8 @@
     y_start("+1", "-0")
     x_start(("x+", "B"), ("x-", "B"), ("z+", "A"), ("z-", "A"))
 
+    own_req.wait()
+    own_bucket.wait()
     for c in range(n_col):
         asked[c : c + 1, :] = jnp.concatenate([req[2 * c : 2 * c + 1, :], req[2 * c + 1 : 2 * c + 2, :]], axis=1)
     requests = asked[...]
@@ -418,6 +422,8 @@
     x_start(("z+", "A", 2), ("z-", "A", 2))
     x_wait(("z+", "fB"), ("z-", "fB"))
     x_start(("x+", "B", 2), ("x-", "B", 2))
+    x_wait(("x+", "fB", 0), ("x-", "fB", 0), ("z+", "fA", 0), ("z-", "fA", 0))
+    some_blocks(block, 9, 11)
     for d in near:
         for way in ("x+", "x-"):
             x_wait((way, "B", d))
@@ -426,8 +432,6 @@
             x_wait((way, "A", d))
             x_start((way, "fA", d))
     some_blocks(block, 5, 9)
-    x_wait(("x+", "fB", 0), ("x-", "fB", 0), ("z+", "fA", 0), ("z-", "fA", 0))
-    some_blocks(block, 9, 11)
     for way in ("x+", "x-"):
         x_wait((way, "B", 2))
         x_start((way, "fB", 2))
@@ -447,12 +451,14 @@
     def column_sums(first, last, start, count):
         def body(q, _):
             at = pl.multiple_of(start + q * 256, 256)
-            total = jnp.zeros((256, rows), F32)
-            for c in range(first, last):
-                total = total + e_buf[c, pl.ds(at, 256), :] * scale[c : c + 1, :]
-            total = total[:, :128] + total[:, 128:]
-            if first > 0:
-                total = total + wide[pl.ds(at, 256), :]
+            total = jnp.zeros((256, 128), F32) if first == 0 else wide[pl.ds(at, 256), :]
+            for c in range(first, last, 2):
+                four = [
+                    e_buf[d, pl.ds(at, 256), h : h + 128] * scale[d : d + 1, h : h + 128]
+                    for d in (c, c + 1)
+                    for h in (0, 128)
+                ]
+                total = total + ((four[0] + four[1]) + (four[2] + four[3]))
             wide[pl.ds(at, 256), :] = total
             return 0
 
@@ -592,9 +598,11 @@
         column_sums(f_half, n_col, half_span, half_span)
         g_leave(it, 1)
         if it < ITERS - 1:
-            for k in range(1 + 5 * it, 6 + 5 * it):
+            for k in col_order[5 * it : 5 * it + 5]:
                 p_copy(k).start()
     cost_b, square_b = unpack(1, flat)
+    leave_i = pltpu.make_async_copy(out_i, out_all, own_sem.at[4])
+    leave_i.start()
     pair_cost = jnp.concatenate([cost_a, cost_b], axis=1)
     norm_x = jnp.concatenate([square_a, square_b], axis=1)
     big_q = jnp.concatenate([g_arrived(ITERS - 1, 0), g_arrived(ITERS - 1, 1)], axis=0)
@@ -634,6 +642,7 @@
     out_w[...] = f_scaled + paired_g + pair_cost / entropic - log_total
     out_bad[0, 0] = jnp.max(jnp.where(arrived == arrived, 0.0, 1.0)).astype(jnp.int32)
 
+    leave_i.wait()
     for move in y_moves:
         y_copy(move, False).wait_send()
     for move in x_moves:
@@ -663,8 +672,8 @@
             jax.ShapeDtypeStruct((1, 1), jnp.int32),
             jax.ShapeDtypeStruct((own_rows, features), BF16),
         ),
-        in_specs=[hbm, hbm, vmem, vmem],
-        out_specs=(vmem,) * 4 + (pl.BlockSpec(memory_space=pltpu.SMEM), vmem),
+        in_specs=[hbm, hbm, hbm, hbm],
+        out_specs=(vmem,) * 4 + (pl.BlockSpec(memory_space=pltpu.SMEM), hbm),
         scratch_shapes=[
             pltpu.VMEM((n_col, own_rows, features), BF16),
             pltpu.VMEM((n_row, own_rows, features), BF16),
@@ -682,7 +691,10 @@
             pltpu.VMEM((2 * n_col, own_rows), F32),
             pltpu.VMEM((2 * n_col, own_rows), F32),
             pltpu.VMEM((n_col, own_rows), jnp.int32),
-            dma((2,)),
+            pltpu.VMEM((2 * n_col, own_rows // 2), jnp.int32),
+            pltpu.VMEM((1, own_rows), jnp.int32),
+            pltpu.VMEM((own_rows, features), BF16),
+            dma((5,)),
             dma((40,)), dma((40,)),
             dma((11,)), dma((11,)),
             dma((ITERS, 2 * n_col)), dma((ITERS, 2 * n_col)),

time: 125 us -> 123 us (0.984)
  Pallas kernels: 121 us -> 119 us
    pallas_call x1, Pallas kernels: 121 us -> 119 us  [shards(): pl.pallas_call(functools.partial(kernel, n_row, n_col, features, total_ro...]
where the time goes in v6:
time: 123 us
  Pallas kernels  119 us (97%)
  between operations  1.35 us (1%)
  other arithmetic  1.26 us (1%)
    pallas_call x1, Pallas kernels, shards(): pl.pallas_call(functools.partial(kernel, n_row, n_col, features, total_ro...  119 us

profile of v6, /device:TPU:1, one launch (start us, length us, event | category | flops | bytes accessed | tf_op | source)
XLA Modules:
  0.0 122.9 jit_solution(146798974784782554)
XLA Ops:
  0.6 119.2 %pairing_plan.1 = (f32[1,256]{1,0:T(1,128)}, f32[1,256]{1,0:T(1,128)}, f32[1,256]{1,0:T(1,128)S(1)}, f32[1,256]{1,0:T(1,128)}, s32[1,1]{1,0:T(1,128)}, /*index=5*/bf16[256,1024]{1,0:T(8,128)(2,1)}) custom-call(bf16[256,1024]{1,0:T(8,128)(2,1)} %lat.1, bf16[256,1024]{1,0:T(8,128)(2,1)} %noi.1, s32[32,128]{1,0:T(8,128)} %bitcast.9, s32[1,256]{1,0:T(1,128)} %bitcast.10), custom_call_target="tpu_custom_call" | custom-call | tf_op jit(solution)/shard_map/pairing_plan/pallas_call | solution.py:668
  120.5 0.0 copy-start.3
  120.5 0.3 conditional.1
  120.8 0.0 copy-start.4
  120.8 1.3 %broadcast_multiply_fusion = (f32[256]{0:T(256)}, f32[256]{0:T(256)}) fusion(f32[256]{0:T(256)} %get-tuple-element.498, f32[256]{0:T(256)} %get-tuple-element.497), kind=kLoop, calls=%fused_computation.24 | loop fusion | flops 512 | bytes 4096 | tf_op jit(solution)/shard_map/mul | solution.py:717
  122.1 0.0 copy-done.3
  122.1 0.8 copy.100
  122.9 0.0 copy-done.4
  (1 shorter events, 0.0 us)
Async XLA Ops:
  120.5 1.6 %copy-start.3 = (bf16[256,1024]{1,0:T(8,128)(2,1)S(1)}, bf16[256,1024]{1,0:T(8,128)(2,1)}, u32[]{:S(2)}) copy-start(bf16[256,1024]{1,0:T(8,128)(2,1)} %get-tuple-element.971) | copy-start | bytes 1572868
  120.8 2.1 %copy-start.4 = (f32[256]{0:T(256)}, f32[256]{0:T(256)S(1)}, u32[]{:S(2)}) copy-start(f32[256]{0:T(256)S(1)} %get-tuple-element.972) | copy-start | bytes 3076

commit v7 on v6

--- a/solution.py
+++ b/solution.py
@@ -129,7 +129,7 @@
 def kernel(
     n_row, n_col, features, total_rows,
     lat, noi, req_in, bucket_in,
-    out_f, out_g, out_w, out_c, out_bad, out_all,
+    out_lines, out_bad, out_all,
     x_buf, y_buf, e_buf, s_buf, norm_y, wide, pick, send_rows, got_rows,
     f_got, g_got, pg_got, peak, scale, rank, asked, req, bucket, out_i,
     own_sem, x_send, x_recv, y_send, y_recv, f_send, f_recv, g_send, g_recv,
@@ -625,9 +625,9 @@
     lse = rank[pl.ds(col, 1), :]
     own_p = rank[pl.ds(n_col + col, 1), :]
     f_scaled = lse / log2e + jnp.log(own_p) + log_total - norm_x / entropic
-    out_f[...] = f_scaled
+    out_lines[0:1, :] = f_scaled
     rank[0:n_row, :] = g
-    out_g[...] = rank[pl.ds(row, 1), :]
+    out_lines[1:2, :] = rank[pl.ds(row, 1), :]
     offset = lax.rem(col, 4) * 32
     grab = (
         lax.broadcasted_iota(jnp.int32, (128, rows), 0).astype(F32) == spot + offset.astype(F32)
@@ -638,8 +638,8 @@
     for part in three_parts(arrived):
         paired_g = paired_g + dot_nn(part, grab)
     paired_g = jnp.sum(jnp.where(marker, paired_g, 0.0), axis=0, keepdims=True)
-    out_c[...] = pair_cost
-    out_w[...] = f_scaled + paired_g + pair_cost / entropic - log_total
+    out_lines[3:4, :] = pair_cost
+    out_lines[2:3, :] = f_scaled + paired_g + pair_cost / entropic - log_total
     out_bad[0, 0] = jnp.max(jnp.where(arrived == arrived, 0.0, 1.0)).astype(jnp.int32)
 
     leave_i.wait()
@@ -663,17 +663,16 @@
     span = own_rows * n_row
     vmem = pl.BlockSpec(memory_space=pltpu.VMEM)
     hbm = pl.BlockSpec(memory_space=pl.ANY)
-    line = jax.ShapeDtypeStruct((1, own_rows), F32)
     dma = pltpu.SemaphoreType.DMA
-    f, g, w, pair_cost, bad, interpolant = pl.pallas_call(
+    lines, bad, interpolant = pl.pallas_call(
         functools.partial(kernel, n_row, n_col, features, total_rows),
         out_shape=(
-            line, line, line, line,
+            jax.ShapeDtypeStruct((4, own_rows), F32),
             jax.ShapeDtypeStruct((1, 1), jnp.int32),
             jax.ShapeDtypeStruct((own_rows, features), BF16),
         ),
         in_specs=[hbm, hbm, hbm, hbm],
-        out_specs=(vmem,) * 4 + (pl.BlockSpec(memory_space=pltpu.SMEM), hbm),
+        out_specs=(vmem, pl.BlockSpec(memory_space=pltpu.SMEM), hbm),
         scratch_shapes=[
             pltpu.VMEM((n_col, own_rows, features), BF16),
             pltpu.VMEM((n_row, own_rows, features), BF16),
@@ -707,14 +706,14 @@
         ),
         name="pairing_plan",
     )(latents, noise, pairing.reshape(2 * n_col, own_rows // 2), time_bucket.reshape(1, own_rows))
+
     def again():
         exact_f, exact_g, paired_g = log_domain(latents, noise, pairing)
-        log_weight = (exact_f + paired_g - pair_cost.reshape(own_rows)) / entropic + math.log(total_rows)
-        return tuple(v.reshape(1, own_rows) for v in (exact_f / -entropic, exact_g / -entropic, -log_weight))
-
-    f, g, w = lax.cond(bad[0, 0] > 0, again, lambda: (f, g, w))
-    f, g, w = (v.reshape(own_rows) for v in (f, g, w))
-    return f * -entropic, g * -entropic, interpolant, -w
+        log_weight = (exact_f + paired_g - lines[3]) / entropic + math.log(total_rows)
+        return jnp.stack([exact_f / -entropic, exact_g / -entropic, -log_weight, lines[3]])
+
+    lines = lax.cond(bad[0, 0] > 0, again, lambda: lines)
+    return lines[0] * -entropic, lines[1] * -entropic, interpolant, -lines[2]
 
 
 def solution(mesh):

time: 123 us -> 122 us (level)
    mul x1 -> x0, other arithmetic: 1.25 us -> none  [shards(): return (f * -entropic, g * -entropic, interpolant, -w)]
where the time goes in v7:
time: 122 us
  Pallas kernels  119 us (98%)
  between operations  1.28 us (1%)
    pallas_call x1, Pallas kernels, shards(): pl.pallas_call(functools.partial(kernel, n_row, n_col, features, total_ro...  119 us

profile of v7, /device:TPU:1, one launch (start us, length us, event | category | flops | bytes accessed | tf_op | source)
XLA Modules:
  0.0 122.1 jit_solution(11779286902869887534)
XLA Ops:
  0.6 119.0 %pairing_plan.1 = (f32[4,256]{1,0:T(4,128)S(1)}, s32[1,1]{1,0:T(1,128)}, bf16[256,1024]{1,0:T(8,128)(2,1)}) custom-call(bf16[256,1024]{1,0:T(8,128)(2,1)} %lat.1, bf16[256,1024]{1,0:T(8,128)(2,1)} %noi.1, s32[32,128]{1,0:T(8,128)} %bitcast.12, s32[1,256]{1,0:T(1,128)} %bitcast.17), custom_call_target="tpu_custom_call" | custom-call | tf_op jit(solution)/shard_map/pairing_plan/pallas_call | solution.py:667
  120.2 0.0 copy-start.3
  120.2 0.3 conditional.1
  120.5 0.6 slice_negate_fusion
  121.1 0.2 copy-done.3
  121.3 0.8 copy.94
Async XLA Ops:
  120.2 1.0 copy-start.3

commit v8 on v7

--- a/solution.py
+++ b/solution.py
@@ -593,13 +593,13 @@
         f_arrived(it, 0)
         column_sums(0, f_half, 0, span)
         f_arrived(it, 1)
+        if it < ITERS - 1:
+            for k in col_order[5 * it : 5 * it + 5]:
+                p_copy(k).start()
         column_sums(f_half, n_col, 0, half_span)
         g_leave(it, 0)
         column_sums(f_half, n_col, half_span, half_span)
         g_leave(it, 1)
-        if it < ITERS - 1:
-            for k in col_order[5 * it : 5 * it + 5]:
-                p_copy(k).start()
     cost_b, square_b = unpack(1, flat)
     leave_i = pltpu.make_async_copy(out_i, out_all, own_sem.at[4])
     leave_i.start()

time: 122 us -> 121 us (level)
  no operation moved by 1% of the time
where the time goes in v8:
time: 121 us
  Pallas kernels  118 us (98%)
  between operations  1.28 us (1%)
    pallas_call x1, Pallas kernels, shards(): pl.pallas_call(functools.partial(kernel, n_row, n_col, features, total_ro...  118 us

profile of v8, /device:TPU:1, one launch (start us, length us, event | category | flops | bytes accessed | tf_op | source)
XLA Modules:
  0.0 120.8 jit_solution(2885568121657408437)
XLA Ops:
  0.6 117.7 %pairing_plan.1 = (f32[4,256]{1,0:T(4,128)S(1)}, s32[1,1]{1,0:T(1,128)}, bf16[256,1024]{1,0:T(8,128)(2,1)}) custom-call(bf16[256,1024]{1,0:T(8,128)(2,1)} %lat.1, bf16[256,1024]{1,0:T(8,128)(2,1)} %noi.1, s32[32,128]{1,0:T(8,128)} %bitcast.12, s32[1,256]{1,0:T(1,128)} %bitcast.17), custom_call_target="tpu_custom_call" | custom-call | tf_op jit(solution)/shard_map/pairing_plan/pallas_call | solution.py:667
  119.0 0.0 copy-start.3
  119.0 0.3 conditional.1
  119.3 0.6 slice_negate_fusion
  119.9 0.2 copy-done.3
  120.0 0.8 copy.94
Async XLA Ops:
  119.0 1.0 copy-start.3
